TPU v7x, 256 devices: a whole 4x4x8 slice. The times are simulated.
256 devices in a mesh: pipe: 8 (over y, z_hi), ep: 32 (over x, z_lo, core).
Axes of the slice: x: 4, y: 4, z: 8 (z_hi: 2, z_lo: 4; z = z_hi * 4 + z_lo), core: 2. Of those that a mesh axis runs over, the one named last changes fastest.
Arguments:
- first_acts: bfloat16 [8, 4096, 4096], P('pipe', 'ep'), may hold values from -6 to 6
- first_routes: int32 [8, 4096, 1], P('pipe', 'ep'), may hold values from 0 to 7; in each aligned block of 128 rows (0 to 127, 128 to 255, ..., all dimensions but the last counted through in order) at most 18 rows name the same one
- first_probs: float32 [8, 4096, 1], P('pipe', 'ep'), may hold values from 0.2 to 2
- second_acts: bfloat16 [8, 4096, 4096], P('pipe', 'ep'), may hold values from -6 to 6
- second_grads: bfloat16 [8, 4096, 4096], P('pipe', 'ep'), may hold values from -6 to 6
- second_routes: int32 [8, 4096, 1], P('pipe', 'ep'), may hold values from 0 to 7; in each aligned block of 128 rows (0 to 127, 128 to 255, ..., all dimensions but the last counted through in order) at most 18 rows name the same one
- second_probs: float32 [8, 4096, 1], P('pipe', 'ep'), may hold values from 0.2 to 2
- gate_weight: bfloat16 [8, 4096, 6144], P('pipe', None, 'ep'), may hold values from -0.09375 to 0.09375
- up_weight: bfloat16 [8, 4096, 6144], P('pipe', None, 'ep'), may hold values from -0.09375 to 0.09375
- down_weight: bfloat16 [8, 6144, 4096], P('pipe', 'ep'), may hold values from -0.21875 to 0.21875
Outputs:
- first_out: bfloat16 [8, 4096, 4096], P('pipe', 'ep')
- input_grads: bfloat16 [8, 4096, 4096], P('pipe', 'ep')
Inputs may be any that keep to these rules, and one draw needn't show every extreme that they name: `first_routes`: within each aligned block of 128 tokens (the tokens of one device) no expert is named more than 18 times, and in every draw some block names some expert exactly 18 times. `second_routes`: as for first_routes.
All inputs are finite; a program needn't handle non-finite values.
Results may differ from a plain program's by a relative error of at most 0.0064.
Values may be sent and summed in bfloat16 or wider, within the bound.
A program may use at most 128 MiB of HBM per device.

v0:
```python
import jax
import jax.numpy as jnp
from jax import lax
from jax.sharding import PartitionSpec as P

SPLIT = 4


def from_behind(array, axis, by):
    size = lax.axis_size(axis)
    return lax.ppermute(array, axis, [(i, (i + by) % size) for i in range(size)])


def expert_forward(rows, gate_part, up_part, down_part):
    gate = jnp.dot(rows, gate_part, preferred_element_type=jnp.float32)
    upper = jnp.dot(rows, up_part, preferred_element_type=jnp.float32)
    hidden = (jax.nn.silu(gate) * upper).astype(jnp.bfloat16)
    return jnp.dot(hidden, down_part, preferred_element_type=jnp.float32).astype(jnp.bfloat16)


def expert_backward(rows, grads, gate_part, up_part, down_part):
    gate = jnp.dot(rows, gate_part, preferred_element_type=jnp.float32)
    upper = jnp.dot(rows, up_part, preferred_element_type=jnp.float32)
    d_hidden = lax.dot_general(
        grads, down_part, (((1,), (1,)), ((), ())), preferred_element_type=jnp.float32
    )
    sig = jax.nn.sigmoid(gate)
    d_gate = (d_hidden * upper * sig * (1.0 + gate * (1.0 - sig))).astype(jnp.bfloat16)
    d_up = (d_hidden * gate * sig).astype(jnp.bfloat16)
    total = lax.dot_general(
        d_gate, gate_part, (((1,), (1,)), ((), ())), preferred_element_type=jnp.float32
    )
    total = total + lax.dot_general(
        d_up, up_part, (((1,), (1,)), ((), ())), preferred_element_type=jnp.float32
    )
    return total.astype(jnp.bfloat16)


def layout(routes, experts, capacity):
    expert = routes[:, 0]
    onehot = (expert[:, None] == jnp.arange(experts, dtype=jnp.int32)[None, :]).astype(jnp.int32)
    before = jnp.cumsum(onehot, axis=0) - onehot
    slot = jnp.sum(before * onehot, axis=1)
    where = expert * capacity + slot
    table = (where[None, :] == jnp.arange(experts * capacity, dtype=jnp.int32)[:, None]).astype(
        jnp.bfloat16
    )
    return (where, table)


def to_buffer(table, values, experts, capacity, split):
    filled = jnp.dot(table, values, preferred_element_type=jnp.float32).astype(jnp.bfloat16)
    filled = filled.reshape(experts, capacity, values.shape[1])
    return jnp.repeat(filled, split, axis=0)


def from_buffer(returned, where, experts, split):
    width = returned.shape[2]
    summed = jnp.sum(returned.reshape(experts, split, -1, width).astype(jnp.float32), axis=1)
    return jnp.take(summed.reshape(-1, width), where, axis=0)


def body(
    first_acts,
    first_routes,
    first_probs,
    second_acts,
    second_grads,
    second_routes,
    second_probs,
    gate_weight,
    up_weight,
    down_weight,
):
    groups = lax.axis_size("ep")
    split = SPLIT
    experts = groups // split
    tok_rows = first_acts.shape[1]
    width = first_acts.shape[2]
    capacity = tok_rows * 9 // (8 * experts)
    gate_part = gate_weight[0]
    up_part = up_weight[0]
    down_part = down_weight[0]
    arrived = from_behind(first_acts[0], "pipe", 1)
    upstream = from_behind(second_grads[0], "pipe", -1)
    where_one, table_one = layout(first_routes[0], experts, capacity)
    where_two, table_two = layout(second_routes[0], experts, capacity)
    scaled = (second_probs[0] * upstream.astype(jnp.float32)).astype(jnp.bfloat16)
    send_one = to_buffer(table_one, arrived, experts, capacity, split)
    landed_one = lax.all_to_all(send_one, "ep", split_axis=0, concat_axis=0, tiled=True)
    send_inputs = to_buffer(table_two, second_acts[0], experts, capacity, split)
    send_grads = to_buffer(table_two, scaled, experts, capacity, split)
    inputs_in, grads_in = (
        lax.all_to_all(send_inputs, "ep", split_axis=0, concat_axis=0, tiled=True),
        lax.all_to_all(send_grads, "ep", split_axis=0, concat_axis=0, tiled=True),
    )
    partial_one = expert_forward(
        landed_one.reshape(-1, width), gate_part, up_part, down_part
    ).reshape(groups, capacity, width)
    flat = expert_backward(
        inputs_in.reshape(-1, width), grads_in.reshape(-1, width), gate_part, up_part, down_part
    )
    partial_two = flat.reshape(groups, capacity, width)
    back_one = lax.all_to_all(partial_one, "ep", split_axis=0, concat_axis=0, tiled=True)
    back_two = lax.all_to_all(partial_two, "ep", split_axis=0, concat_axis=0, tiled=True)
    first_out = (first_probs[0] * from_buffer(back_one, where_one, experts, split)).astype(
        jnp.bfloat16
    )
    input_grads = from_buffer(back_two, where_two, experts, split).astype(jnp.bfloat16)
    return (first_out[None], input_grads[None])


def solution(mesh):
    in_specs = (
        P("pipe", "ep", None),
        P("pipe", "ep", None),
        P("pipe", "ep", None),
        P("pipe", "ep", None),
        P("pipe", "ep", None),
        P("pipe", "ep", None),
        P("pipe", "ep", None),
        P("pipe", None, "ep"),
        P("pipe", None, "ep"),
        P("pipe", "ep", None),
    )
    out_specs = (P("pipe", "ep", None), P("pipe", "ep", None))
    return jax.shard_map(body, mesh=mesh, in_specs=in_specs, out_specs=out_specs, check_vma=False)
```

profile of v0, /device:TPU:7, one launch (start us, length us, event | category | flops | bytes accessed | tf_op | source)
XLA Modules:
  0.0 855.5 jit_solution(12288929835535395022)
XLA Ops:
  0.6 0.9 fusion.52
  1.5 0.2 reduce_window_sum.18
  1.7 0.8 select_reduce_fusion
  2.5 0.7 compare_and_fusion
  3.2 2.7 convolution_convert_fusion.1
  5.9 1.4 reshape.82
  7.3 3.4 broadcast_in_dim.33
  10.8 9.5 %all-to-all-start.3 = ((bf16[32,18,4096]{2,1,0:T(8,128)(2,1)}), bf16[32,18,4096]{2,1,0:T(8,128)(2,1)}, u32[]{:S(2)}, u32[]{:S(2)}) async-start(bf16[32,18,4096]{2,1,0:T(8,128)(2,1)} %bitcast.67), calls=%async_computation.3 | async-start | bytes 12582912 | tf_op jit(solution)/shard_map/all_to_all | solution.py:94
  20.3 4.3 collective-permute-start
  24.7 0.2 reduce_window_sum.17
  24.9 0.2 select_reduce_fusion.1
  25.1 150.3 %collective-permute-done = bf16[128,4096]{1,0:T(8,128)(2,1)S(1)} collective-permute-done((bf16[128,4096]{1,0:T(8,128)(2,1)}, bf16[128,4096]{1,0:T(8,128)(2,1)S(1)}, u32[]{:S(2)}, u32[]{:S(2)}) %collective-permute-start) | collective-permute-done | bytes 1048608 | tf_op jit(solution)/shard_map/ppermute | solution.py:11
  175.4 1.6 convolution_convert_fusion.3
  176.9 1.4 reshape.74
  178.4 25.3 %all-to-all-done.3 = bf16[32,18,4096]{2,1,0:T(8,128)(2,1)} async-done(((bf16[32,18,4096]{2,1,0:T(8,128)(2,1)}), bf16[32,18,4096]{2,1,0:T(8,128)(2,1)}, u32[]{:S(2)}, u32[]{:S(2)}) %all-to-all-start.3) | async-done | bytes 4718624 | tf_op jit(solution)/shard_map/all_to_all | solution.py:94
  203.7 3.4 broadcast_in_dim.30
  207.1 6.9 all-to-all-start
  214.1 6.7 collective-permute-start.1
  220.8 145.9 %collective-permute-done.1 = bf16[128,4096]{1,0:T(8,128)(2,1)S(1)} collective-permute-done((bf16[128,4096]{1,0:T(8,128)(2,1)S(1)}, bf16[128,4096]{1,0:T(8,128)(2,1)S(1)}, u32[]{:S(2)}, u32[]{:S(2)}) %collective-permute-start.1) | collective-permute-done | bytes 1048608 | tf_op jit(solution)/shard_map/ppermute | solution.py:11
  366.7 1.6 convolution_convert_fusion.2
  368.3 1.4 reshape.79
  369.7 27.7 %all-to-all-done = bf16[32,18,4096]{2,1,0:T(8,128)(2,1)} async-done(((bf16[32,18,4096]{2,1,0:T(8,128)(2,1)}), bf16[32,18,4096]{2,1,0:T(8,128)(2,1)}, u32[]{:S(2)}, u32[]{:S(2)}) %all-to-all-start) | async-done | bytes 4718624 | tf_op jit(solution)/shard_map/all_to_all | solution.py:90
  397.4 3.4 broadcast_in_dim.32
  400.8 6.9 all-to-all-start.2
  407.7 7.9 reshape.76
  415.6 5.0 fusion.13
  420.6 9.3 %convolution_convert_fusion = bf16[576,4096]{1,0:T(8,128)(2,1)} fusion(bf16[1,192,4096]{2,1,0:T(8,128)(2,1)} %param.21, bf16[576,4096]{1,0:T(8,128)(2,1)} %reshape.76, bf16[1,4096,192]{1,2,0:T(8,128)(2,1)S(1)} %copy-done, f32[576,192]{0,1:T(8,128)} %fusion.13), kind=kOutput, calls=%fused_computation.5 | convolution fusion | flops 1814962176 | bytes 13025280 | tf_op jit(solution)/shard_map/dot_general | solution.py:18
  429.8 7.6 reshape.77
  437.4 108.6 %all-to-all-done.2 = bf16[32,18,4096]{2,1,0:T(8,128)(2,1)} async-done(((bf16[32,18,4096]{2,1,0:T(8,128)(2,1)}), bf16[32,18,4096]{2,1,0:T(8,128)(2,1)}, u32[]{:S(2)}, u32[]{:S(2)}) %all-to-all-start.2) | async-done | bytes 4718624 | tf_op jit(solution)/shard_map/all_to_all | solution.py:95
  546.1 7.0 all-to-all-start.1
  553.1 7.8 reshape.84
  560.9 4.7 fusion.11
  565.6 7.7 reshape.81
  573.3 4.7 fusion.1
  578.0 10.6 %fusion.9 = f32[576,4096]{1,0:T(8,128)} fusion(bf16[1,4096,192]{1,2,0:T(8,128)(2,1)} %param.19, f32[576,192]{0,1:T(8,128)S(1)} %fusion.1, bf16[576,4096]{1,0:T(8,128)(2,1)} %reshape.84, bf16[1,4096,192]{1,2,0:T(8,128)(2,1)S(1)} %copy-done, f32[576,192]{0,1:T(8,128)S(1)} %fusion.11), kind=kOutput, calls=%fused_computation.21 | convolution fusion | flops 1813045248 | bytes 18186240 | tf_op jit(solution)/shard_map/dot_general | solution.py:30
  588.6 7.3 add_convert_fusion
  595.9 7.6 reshape.85
  603.5 88.0 %all-to-all-done.1 = bf16[32,18,4096]{2,1,0:T(8,128)(2,1)} async-done(((bf16[32,18,4096]{2,1,0:T(8,128)(2,1)}), bf16[32,18,4096]{2,1,0:T(8,128)(2,1)}, u32[]{:S(2)}, u32[]{:S(2)}) %all-to-all-start.1) | async-done | bytes 4718624 | tf_op jit(solution)/shard_map/all_to_all | solution.py:104
  691.5 6.9 all-to-all-start.4
  698.4 6.0 convert_reduce_fusion.1
  704.5 3.1 reshape.78
  707.6 129.4 %all-to-all-done.4 = bf16[32,18,4096]{2,1,0:T(8,128)(2,1)} async-done(((bf16[32,18,4096]{2,1,0:T(8,128)(2,1)}), bf16[32,18,4096]{2,1,0:T(8,128)(2,1)}, u32[]{:S(2)}, u32[]{:S(2)}) %all-to-all-start.4) | async-done | bytes 4718624 | tf_op jit(solution)/shard_map/all_to_all | solution.py:105
  837.0 5.7 convert_reduce_fusion
  842.7 1.6 reshape.86
  844.3 5.1 gather_fusion
  849.4 2.2 gather_fusion.1
  851.6 2.6 fusion.38
  854.2 1.3 fusion.37
  (20 shorter events, 0.1 us)
Async XLA Ops:
  0.6 419.9 %copy-start = (bf16[1,4096,192]{1,2,0:T(8,128)(2,1)S(1)}, bf16[1,4096,192]{1,2,0:T(8,128)(2,1)}, u32[]{:S(2)}) copy-start(bf16[1,4096,192]{1,2,0:T(8,128)(2,1)} %param.20) | copy-start | bytes 4718596
  10.8 13.8 %copy-start.3 = (s32[1,128,1]{1,2,0:T(1,128)S(1)}, s32[1,128,1]{1,2,0:T(1,128)}, u32[]{:S(2)}) copy-start(s32[1,128,1]{1,2,0:T(1,128)} %param.13) | copy-start | bytes 1540
  10.8 192.9 %all-to-all-start.3 = ((bf16[32,18,4096]{2,1,0:T(8,128)(2,1)}), bf16[32,18,4096]{2,1,0:T(8,128)(2,1)}, u32[]{:S(2)}, u32[]{:S(2)}) async-start(bf16[32,18,4096]{2,1,0:T(8,128)(2,1)} %bitcast.67), calls=%async_computation.3 | async-start | bytes 12582912 | tf_op jit(solution)/shard_map/all_to_all | solution.py:94
  20.3 155.1 %collective-permute-start = (bf16[128,4096]{1,0:T(8,128)(2,1)}, bf16[128,4096]{1,0:T(8,128)(2,1)S(1)}, u32[]{:S(2)}, u32[]{:S(2)}) collective-permute-start(bf16[128,4096]{1,0:T(8,128)(2,1)} %bitcast.76), channel_id=1, source_target_pairs={{0,32},{32,64},{64,96},{96,128},{128,160},{160,192},{192,224},{224... | collective-permute-start | bytes 3145736 | tf_op jit(solution)/shard_map/ppermute | solution.py:11
  207.1 6.9 copy-start.6
  207.1 159.5 %copy-start.5 = (f32[1,128,1]{1,2,0:T(1,128)S(1)}, f32[1,128,1]{1,2,0:T(1,128)}, u32[]{:S(2)}) copy-start(f32[1,128,1]{1,2,0:T(1,128)} %param.18) | copy-start | bytes 1540
  207.1 190.3 %all-to-all-start = ((bf16[32,18,4096]{2,1,0:T(8,128)(2,1)}), bf16[32,18,4096]{2,1,0:T(8,128)(2,1)}, u32[]{:S(2)}, u32[]{:S(2)}) async-start(bf16[32,18,4096]{2,1,0:T(8,128)(2,1)} %bitcast.68), calls=%async_computation | async-start | bytes 12582912 | tf_op jit(solution)/shard_map/all_to_all | solution.py:90
  214.1 152.6 %collective-permute-start.1 = (bf16[128,4096]{1,0:T(8,128)(2,1)S(1)}, bf16[128,4096]{1,0:T(8,128)(2,1)S(1)}, u32[]{:S(2)}, u32[]{:S(2)}) collective-permute-start(bf16[128,4096]{1,0:T(8,128)(2,1)S(1)} %bitcast.77), channel_id=1, source_target_pairs={{0,224},{32,0},{64,32},{96,64},{128,96},{160,128},{192,160},{224,1... | collective-permute-start | bytes 3145736 | tf_op jit(solution)/shard_map/ppermute | solution.py:11
  400.8 145.2 %all-to-all-start.2 = ((bf16[32,18,4096]{2,1,0:T(8,128)(2,1)}), bf16[32,18,4096]{2,1,0:T(8,128)(2,1)}, u32[]{:S(2)}, u32[]{:S(2)}) async-start(bf16[32,18,4096]{2,1,0:T(8,128)(2,1)} %bitcast.69), calls=%async_computation.2 | async-start | bytes 12582912 | tf_op jit(solution)/shard_map/all_to_all | solution.py:95
  407.7 7.9 copy-start.2
  546.1 145.4 %all-to-all-start.1 = ((bf16[32,18,4096]{2,1,0:T(8,128)(2,1)}), bf16[32,18,4096]{2,1,0:T(8,128)(2,1)}, u32[]{:S(2)}, u32[]{:S(2)}) async-start(bf16[32,18,4096]{2,1,0:T(8,128)(2,1)} %reshape.77), calls=%async_computation.1 | async-start | bytes 12582912 | tf_op jit(solution)/shard_map/all_to_all | solution.py:104
  691.5 145.5 %all-to-all-start.4 = ((bf16[32,18,4096]{2,1,0:T(8,128)(2,1)}), bf16[32,18,4096]{2,1,0:T(8,128)(2,1)}, u32[]{:S(2)}, u32[]{:S(2)}) async-start(bf16[32,18,4096]{2,1,0:T(8,128)(2,1)} %reshape.85), calls=%async_computation.4 | async-start | bytes 12582912 | tf_op jit(solution)/shard_map/all_to_all | solution.py:105
  851.6 2.6 copy-start.1
  851.6 2.6 copy-start.4
where the time goes:
time: 858 us; the launch traced here: 855 us
  waiting for transfers between devices  675 us (79%)
  local copies, waits for them, and re-layouts  65.1 us (8%)
  starting transfers between devices  48.2 us (6%)
  matrix products  47.4 us (6%)
  other arithmetic  18.6 us (2%)
    ppermute x2, waiting for transfers between devices, from_behind(): lax.ppermute(array, axis, [(i, (i + by) % size) for i in range(size)])  296 us
    all_to_all x1, waiting for transfers between devices, body(): lax.all_to_all(partial_two, 'ep', split_axis=0, concat_axis=0, tiled=True)  129 us
    all_to_all x1, waiting for transfers between devices, body(): lax.all_to_all(send_grads, 'ep', split_axis=0, concat_axis=0, tiled=True)  109 us
    all_to_all x1, waiting for transfers between devices, body(): lax.all_to_all(partial_one, 'ep', split_axis=0, concat_axis=0, tiled=True)  88 us
    all_to_all x1, waiting for transfers between devices, body(): lax.all_to_all(send_one, 'ep', split_axis=0, concat_axis=0, tiled=True)  27.7 us
    all_to_all x1, waiting for transfers between devices, body(): lax.all_to_all(send_inputs, 'ep', split_axis=0, concat_axis=0, tiled=True)  25.3 us
  transfers between devices with their start and end apart: 7, of which 7 were waited for; matrix products, arithmetic and copies ran while one was open for 11% of the time, Pallas kernels for 0%

commit v1 on v0

v1 whole, which is shorter than its diff:
```python
import jax
import jax.numpy as jnp
from jax import lax
from jax.experimental import pallas as pl
from jax.experimental.pallas import tpu as pltpu
from jax.sharding import PartitionSpec as P

MESH = pl.DeviceIdType.MESH
F32 = jnp.float32
BF16 = jnp.bfloat16
NT = (((1,), (1,)), ((), ()))

TOK = 128
D = 4096
HID = 192
EXPERTS = 8
KB = 512
NK = D // KB
W = D + KB
BLK = 16
SRC = 32
MAIN = SRC * BLK
EXTRA = SRC * 2
ROWS = MAIN + EXTRA
SECTIONS = 8

ONE, ACTS, GRADS = 0, 1, 2


def rows16(index):
    return pl.ds(pl.multiple_of(index * BLK, BLK), BLK)


def cols(index):
    return pl.ds(pl.multiple_of(index * KB, KB), KB)


def iota(shape, dim):
    return lax.broadcasted_iota(jnp.int32, shape, dim)


def onehot(mask):
    return jnp.where(mask, 1.0, 0.0).astype(BF16)


def codes(expert_col):
    here, there = iota((TOK, TOK), 0), iota((TOK, TOK), 1)
    col = jnp.broadcast_to(expert_col.astype(F32), (TOK, TOK))
    row = jnp.sum(jnp.where(here == there, col, 0.0), axis=0, keepdims=True)
    same = jnp.where(col == row, 1.0, 0.0)
    slot_col = jnp.sum(jnp.where(there < here, same, 0.0), axis=1, keepdims=True)
    slot_row = jnp.sum(jnp.where(here < there, same, 0.0), axis=0, keepdims=True)

    def both(expert, slot):
        main = jnp.where(slot < BLK, expert * BLK + slot, -1.0)
        tail = jnp.where(slot < BLK, -1024.0, expert * BLK + slot - BLK)
        return main, tail

    return both(col[:, 0:1], slot_col), both(row, slot_row)


def entry_own(z, q):
    return jnp.where(q == 0, jnp.minimum(z, 1), jnp.maximum(z, 2))


def entry_far(z, q):
    return jnp.where(q == 0, jnp.where(z == 0, 1, 0), jnp.where(z == 3, 2, 3))


def kernel(
    routes_one, probs_one, routes_two, probs_two, one_hbm, acts_hbm, grads_hbm, gate_hbm, up_hbm, down_hbm,
    out_one, out_two,
    held, wg, wu, wd, meta_out, meta_in, stage, recv, part, cx, px, home, acc, hid,
    load_sem, msend, mrecv, dsend, fsend, csend, rsem, xsend, xrecv, psend, precv, hsend, hrecv,
):
    p, j = lax.axis_index("pipe"), lax.axis_index("ep")
    x, z, c = j // 8, (j // 2) % 4, j % 2
    q = z // 2
    expert = j // 4
    mine = c * 16 + x * 4 + z
    other = x * 8 + z * 2 + (1 - c)
    pair = x * 8 + (q * 4 + 1 - z) * 2 + c
    after, before = lax.rem(p + 1, SECTIONS), lax.rem(p + SECTIONS - 1, SECTIONS)
    section = {ONE: after, ACTS: p, GRADS: before}

    def entry(d, source_z, pair_index):
        return entry_own(source_z, pair_index) if d == ACTS else entry_far(source_z, pair_index)

    loads = [
        pltpu.make_async_copy(src, dst, load_sem.at[i])
        for i, (src, dst) in enumerate(
            [
                (acts_hbm, held.at[ACTS]),
                (one_hbm, held.at[ONE]),
                (grads_hbm, held.at[GRADS]),
                (gate_hbm, wg),
                (up_hbm, wu),
                (down_hbm, wd),
            ]
        )
    ]
    for load in loads:
        load.start()

    barrier = pltpu.get_barrier_semaphore()

    def greet(n, carry):
        them = (n // 4) * 8 + (n % 4) * 2 + c
        pl.semaphore_signal(barrier, inc=1, device_id=(after, them), device_id_type=MESH)
        pl.semaphore_signal(barrier, inc=1, device_id=(before, them), device_id_type=MESH)

        @pl.when(them != j)
        def _():
            pl.semaphore_signal(barrier, inc=1, device_id=(p, them), device_id_type=MESH)

        return carry

    lax.fori_loop(0, 16, greet, 0)
    pl.semaphore_signal(barrier, inc=1, device_id=(p, other), device_id_type=MESH)

    (main_col_one, tail_col_one), (main_row_one, tail_row_one) = codes(routes_one[...])
    (main_col_two, tail_col_two), (main_row_two, tail_row_two) = codes(routes_two[...])
    eye = iota((TOK, TOK), 0) == iota((TOK, TOK), 1)
    prob_row_two = jnp.sum(jnp.where(eye, jnp.broadcast_to(probs_two[...], (TOK, TOK)), 0.0), axis=0, keepdims=True)
    meta_out[0, 0:1, :] = main_row_one
    meta_out[0, 1:2, :] = tail_row_one
    meta_out[0, 2:8, :] = jnp.zeros((6, TOK), F32)
    meta_out[1, 0:1, :] = main_row_two
    meta_out[1, 1:2, :] = tail_row_two
    meta_out[1, 2:3, :] = prob_row_two
    meta_out[1, 3:8, :] = jnp.zeros((5, TOK), F32)

    pl.semaphore_wait(barrier, 48)

    metas = [
        pltpu.make_async_remote_copy(
            meta_out.at[i], meta_in.at[i], msend.at[i], mrecv.at[i], device_id=(to, j), device_id_type=MESH
        )
        for i, to in enumerate((before, after))
    ]
    for copy in metas:
        copy.start()

    def fill(d, main_row, tail_row, prob_row):
        row = iota((TOK, TOK), 0).astype(F32)
        here = row == main_row
        table = onehot(here)
        tail = jnp.zeros((TOK, KB), F32)
        tail_prob = jnp.zeros((TOK, 1), F32)
        if prob_row is not None:
            prob = jnp.sum(jnp.where(here, prob_row, 0.0), axis=1, keepdims=True)
        for k in range(NK):
            values = held[d, :, k * KB : (k + 1) * KB]
            got = jnp.dot(table, values, preferred_element_type=F32)
            there = row == tail_row + 2.0 * k
            tail = tail + jnp.dot(onehot(there), values, preferred_element_type=F32)
            if prob_row is not None:
                got = prob * got
                tail_prob = tail_prob + jnp.sum(jnp.where(there, prob_row, 0.0), axis=1, keepdims=True)
            stage[d, :, k * KB : (k + 1) * KB] = got.astype(BF16)
        if prob_row is not None:
            tail = tail_prob * tail
        stage[d, :, D:W] = tail.astype(BF16)

    def dispatch(d, e):
        target = (e // 2) * 8 + entry(d, z, e % 2) * 2 + c
        return target, pltpu.make_async_remote_copy(
            stage.at[d, rows16(e)],
            recv.at[d, rows16(mine)],
            dsend.at[d, e],
            rsem.at[d, mine],
            device_id=(section[d], target),
            device_id_type=MESH,
        )

    def send_all(d):
        def step(n, carry):
            e = lax.rem(x * 2 + n, EXPERTS)
            target, copy = dispatch(d, e)
            if d == ACTS:
                pl.when(target != j)(copy.start)

                @pl.when(target == j)
                def _():
                    pltpu.make_async_copy(stage.at[d, rows16(e)], recv.at[d, rows16(mine)], rsem.at[d, mine]).start()
            else:
                copy.start()
            return carry

        lax.fori_loop(0, EXPERTS, step, 0)

    def arrived(d, b):
        pltpu.make_async_copy(recv.at[d, rows16(b)], recv.at[d, rows16(b)], rsem.at[d, b]).wait()

    def onward(d, n, to, sem):
        b = c * 16 + n
        return pltpu.make_async_remote_copy(
            recv.at[d, rows16(b)],
            recv.at[d, rows16(b)],
            sem.at[d, n],
            rsem.at[d, b],
            device_id=(p, to),
            device_id_type=MESH,
        )

    def forward(d, direct):
        def step(n, carry):
            enters = entry(d, n % 4, q) == z

            @pl.when(enters if direct else jnp.logical_not(enters))
            def _():
                arrived(d, c * 16 + n)
                if direct:
                    onward(d, n, pair, fsend).start()
                onward(d, n, other, csend).start()

            return carry

        lax.fori_loop(0, 16, step, 0)

    def from_core(d):
        def step(n, carry):
            arrived(d, (1 - c) * 16 + n)
            return carry

        lax.fori_loop(0, 16, step, 0)

    def unfold(d):
        row, col = iota((EXTRA, MAIN), 0), iota((EXTRA, MAIN), 1)
        base = (row // 2) * BLK + row % 2
        tail = recv[d, 0:MAIN, D:W]
        for k in range(NK):
            pick = onehot(col == base + 2 * k)
            recv[d, MAIN:ROWS, k * KB : (k + 1) * KB] = jnp.dot(pick, tail, preferred_element_type=F32).astype(BF16)

    def fold(m):
        row, col = iota((MAIN, EXTRA), 0), iota((MAIN, EXTRA), 1)
        base = (col // 2) * BLK + col % 2
        tail = jnp.zeros((MAIN, KB), F32)
        for k in range(NK):
            pick = onehot(row == base + 2 * k)
            tail = tail + jnp.dot(pick, part[m, MAIN:ROWS, k * KB : (k + 1) * KB], preferred_element_type=F32)
        part[m, 0:MAIN, D:W] = tail.astype(BF16)

    def gate_up(d):
        acc[0:2] = jnp.zeros((2, ROWS, HID), F32)

        def step(k, carry):
            values = recv[d, :, cols(k)]
            acc[0] += jnp.dot(values, wg[cols(k), :], preferred_element_type=F32)
            acc[1] += jnp.dot(values, wu[cols(k), :], preferred_element_type=F32)
            return carry

        lax.fori_loop(0, NK, step, 0)

    def forward_compute():
        unfold(ONE)
        gate_up(ONE)
        gate = acc[0]
        hid[0] = (gate * jax.nn.sigmoid(gate) * acc[1]).astype(BF16)

        def step(k, carry):
            part[0, :, cols(k)] = jnp.dot(hid[0], wd[:, cols(k)], preferred_element_type=F32).astype(BF16)
            return carry

        lax.fori_loop(0, NK, step, 0)
        fold(0)

    def backward_compute():
        unfold(GRADS)
        acc[2] = jnp.zeros((ROWS, HID), F32)

        def down(k, carry):
            acc[2] += lax.dot_general(recv[GRADS, :, cols(k)], wd[:, cols(k)], NT, preferred_element_type=F32)
            return carry

        lax.fori_loop(0, NK, down, 0)
        gate = acc[0]
        sig = jax.nn.sigmoid(gate)
        slope = acc[2] * sig
        hid[0] = (slope * acc[1] * (1.0 + gate * (1.0 - sig))).astype(BF16)
        hid[1] = (slope * gate).astype(BF16)

        def step(k, carry):
            total = lax.dot_general(hid[0], wg[cols(k), :], NT, preferred_element_type=F32)
            total = total + lax.dot_general(hid[1], wu[cols(k), :], NT, preferred_element_type=F32)
            part[1, :, cols(k)] = total.astype(BF16)
            return carry

        lax.fori_loop(0, NK, step, 0)
        fold(1)

    def to_core(m, g):
        quarter = pl.ds(pl.multiple_of((1 - c) * 256 + g * 64, 64), 64)
        return pltpu.make_async_remote_copy(
            part.at[m, quarter],
            cx.at[m, pl.ds(g * 64, 64)],
            xsend.at[m, g],
            xrecv.at[m, g],
            device_id=(p, other),
            device_id_type=MESH,
        )

    def add_into(m, n, ref):
        b = rows16(c * 16 + n)
        part[m, b, :] = (part[m, b, :].astype(F32) + ref[m, rows16(n), :].astype(F32)).astype(BF16)

    def to_pair(m, n):
        return pltpu.make_async_remote_copy(
            part.at[m, rows16(c * 16 + n)],
            px.at[m, rows16(n)],
            psend.at[m, n],
            precv.at[m, n],
            device_id=(p, pair),
            device_id_type=MESH,
        )

    def to_home(m, n):
        target = (n // 4) * 8 + (n % 4) * 2 + c
        return target, pltpu.make_async_remote_copy(
            part.at[m, rows16(c * 16 + n)],
            home.at[m, rows16(expert)],
            hsend.at[m, n],
            hrecv.at[m, expert],
            device_id=(p, target),
            device_id_type=MESH,
        )

    def leaves_here(n):
        return entry_own(n % 4, q) == z

    def return_first(m):
        for g in range(4):
            pltpu.make_async_copy(cx.at[m, pl.ds(g * 64, 64)], cx.at[m, pl.ds(g * 64, 64)], xrecv.at[m, g]).wait()

            def step(n, carry):
                add_into(m, n, cx)

                @pl.when(jnp.logical_not(leaves_here(n)))
                def _():
                    to_pair(m, n).start()

                return carry

            lax.fori_loop(g * 4, g * 4 + 4, step, 0)

    def return_second(m):
        def step(n, carry):
            @pl.when(leaves_here(n))
            def _():
                pltpu.make_async_copy(px.at[m, rows16(n)], px.at[m, rows16(n)], precv.at[m, n]).wait()
                add_into(m, n, px)
                target, copy = to_home(m, n)
                pl.when(target != j)(copy.start)

                @pl.when(target == j)
                def _():
                    pltpu.make_async_copy(
                        part.at[m, rows16(c * 16 + n)], home.at[m, rows16(expert)], hrecv.at[m, expert]
                    ).start()

            return carry

        lax.fori_loop(0, 16, step, 0)

    def collect(m, main_col, tail_col, prob_col, out):
        def step(e, carry):
            pltpu.make_async_copy(home.at[m, rows16(e)], home.at[m, rows16(e)], hrecv.at[m, e]).wait()
            return carry

        lax.fori_loop(0, EXPERTS, step, 0)
        row = iota((TOK, TOK), 1).astype(F32)
        table = onehot(row == main_col)
        tail = home[m, :, D:W]
        for k in range(NK):
            got = jnp.dot(table, home[m, :, k * KB : (k + 1) * KB], preferred_element_type=F32)
            got = got + jnp.dot(onehot(row == tail_col + 2.0 * k), tail, preferred_element_type=F32)
            if prob_col is not None:
                got = prob_col * got
            out[:, k * KB : (k + 1) * KB] = got.astype(BF16)

    loads[0].wait()
    fill(ACTS, main_row_two, tail_row_two, None)
    send_all(ACTS)
    loads[1].wait()
    metas[0].wait_recv()
    fill(ONE, meta_in[0, 0:1, :], meta_in[0, 1:2, :], None)
    send_all(ONE)
    loads[2].wait()
    metas[1].wait_recv()
    fill(GRADS, meta_in[1, 0:1, :], meta_in[1, 1:2, :], meta_in[1, 2:3, :])
    send_all(GRADS)

    forward(ACTS, True)
    forward(ONE, True)
    forward(ACTS, False)
    forward(ONE, False)
    from_core(ONE)
    for load in loads[3:]:
        load.wait()
    forward_compute()
    for g in range(4):
        to_core(0, g).start()
    from_core(ACTS)
    unfold(ACTS)
    gate_up(ACTS)
    return_first(0)
    forward(GRADS, True)
    return_second(0)
    forward(GRADS, False)
    from_core(GRADS)
    backward_compute()
    for g in range(4):
        to_core(1, g).start()
    collect(0, main_col_one, tail_col_one, probs_one[...], out_one)
    return_first(1)
    return_second(1)
    collect(1, main_col_two, tail_col_two, None, out_two)

    for copy in metas:
        copy.wait_send()

    for d in (ACTS, ONE, GRADS):

        def sent(e, carry):
            target, copy = dispatch(d, e)
            if d == ACTS:
                pl.when(target != j)(copy.wait_send)
            else:
                copy.wait_send()
            return carry

        lax.fori_loop(0, EXPERTS, sent, 0)

        def passed(n, carry):
            @pl.when(entry(d, n % 4, q) == z)
            def _():
                onward(d, n, pair, fsend).wait_send()

            onward(d, n, other, csend).wait_send()
            return carry

        lax.fori_loop(0, 16, passed, 0)

    for m in range(2):
        for g in range(4):
            to_core(m, g).wait_send()

        def returned(n, carry):
            leaves = leaves_here(n)

            @pl.when(jnp.logical_not(leaves))
            def _():
                to_pair(m, n).wait_send()

            target, copy = to_home(m, n)
            pl.when(jnp.logical_and(leaves, target != j))(copy.wait_send)
            return carry

        lax.fori_loop(0, 16, returned, 0)


def body(
    first_acts,
    first_routes,
    first_probs,
    second_acts,
    second_grads,
    second_routes,
    second_probs,
    gate_weight,
    up_weight,
    down_weight,
):
    vmem = pl.BlockSpec(memory_space=pltpu.VMEM)
    hbm = pl.BlockSpec(memory_space=pl.ANY)
    dma = pltpu.SemaphoreType.DMA
    result = jax.ShapeDtypeStruct((TOK, D), BF16)
    first_out, input_grads = pl.pallas_call(
        kernel,
        out_shape=(result, result),
        in_specs=[vmem] * 4 + [hbm] * 6,
        out_specs=(vmem, vmem),
        scratch_shapes=[
            pltpu.VMEM((3, TOK, D), BF16),
            pltpu.VMEM((D, HID), BF16),
            pltpu.VMEM((D, HID), BF16),
            pltpu.VMEM((HID, D), BF16),
            pltpu.VMEM((2, 8, TOK), F32),
            pltpu.VMEM((2, 8, TOK), F32),
            pltpu.VMEM((3, EXPERTS * BLK, W), BF16),
            pltpu.VMEM((3, ROWS, W), BF16),
            pltpu.VMEM((2, ROWS, W), BF16),
            pltpu.VMEM((2, MAIN // 2, W), BF16),
            pltpu.VMEM((2, MAIN // 2, W), BF16),
            pltpu.VMEM((2, EXPERTS * BLK, W), BF16),
            pltpu.VMEM((3, ROWS, HID), F32),
            pltpu.VMEM((2, ROWS, HID), BF16),
            dma((6,)),
            dma((2,)),
            dma((2,)),
            dma((3, EXPERTS)),
            dma((3, 16)),
            dma((3, 16)),
            dma((3, SRC)),
            dma((2, 4)),
            dma((2, 4)),
            dma((2, 16)),
            dma((2, 16)),
            dma((2, 16)),
            dma((2, EXPERTS)),
        ],
        compiler_params=pltpu.CompilerParams(
            collective_id=0, has_side_effects=True, vmem_limit_bytes=63 * 1024 * 1024
        ),
    )(
        first_routes[0],
        first_probs[0],
        second_routes[0],
        second_probs[0],
        first_acts[0],
        second_acts[0],
        second_grads[0],
        gate_weight[0],
        up_weight[0],
        down_weight[0],
    )
    return (first_out[None], input_grads[None])


def solution(mesh):
    in_specs = (
        P("pipe", "ep", None),
        P("pipe", "ep", None),
        P("pipe", "ep", None),
        P("pipe", "ep", None),
        P("pipe", "ep", None),
        P("pipe", "ep", None),
        P("pipe", "ep", None),
        P("pipe", None, "ep"),
        P("pipe", None, "ep"),
        P("pipe", "ep", None),
    )
    out_specs = (P("pipe", "ep", None), P("pipe", "ep", None))
    return jax.shard_map(body, mesh=mesh, in_specs=in_specs, out_specs=out_specs, check_vma=False)
```

time: 858 us -> 286 us (0.33)
  waiting for transfers between devices: 675 us -> 0 us
  Pallas kernels: 0 us -> 267 us
  local copies, waits for them, and re-layouts: 65.1 us -> 15.3 us
  starting transfers between devices: 48.2 us -> 0 us
  matrix products: 47.4 us -> 0 us
  other arithmetic: 18.6 us -> 0 us
    all_to_all x5 -> x0, waiting for transfers between devices: 379 us -> none  [the longest x1 129 us: body(): lax.all_to_all(partial_two, 'ep', split_axis=0, concat_axis=0, tiled=True)]
    ppermute x2 -> x0, waiting for transfers between devices: 296 us -> none  [from_behind(): lax.ppermute(array, axis, [(i, (i + by) % size) for i in range(size)])]
    pallas_call x0 -> x1, Pallas kernels: none -> 267 us  [body(): pl.pallas_call(kernel, out_shape=(result, result), in_specs=[vmem] * 4 +...]
    reshape x10 -> x0, local copies, waits for them, and re-layouts: 47.5 us -> none  [the longest x1 7.87 us: body(): landed_one.reshape(-1, width)]
    dot_general x9 -> x0, matrix products: 47.4 us -> none  [the longest x1 10.6 us: expert_backward(): lax.dot_general(d_gate, gate_part, (((1,), (1,)), ((), ())), preferred_el...]
    all_to_all x5 -> x0, starting transfers between devices: 37.2 us -> none  [the longest x1 9.54 us: body(): lax.all_to_all(send_inputs, 'ep', split_axis=0, concat_axis=0, tiled=True)]
    reduce_sum x4 -> x0, other arithmetic: 12.8 us -> none  [the longest x2 11.8 us: from_buffer(): jnp.sum(returned.reshape(experts, split, -1, width).astype(jnp.float32),...]
    ppermute x2 -> x0, starting transfers between devices: 11 us -> none  [from_behind(): lax.ppermute(array, axis, [(i, (i + by) % size) for i in range(size)])]
  transfers between devices with their start and end apart: 7 -> 0, of which waited for: 7 -> 0; matrix products, arithmetic and copies ran while one was open for 11% -> 0% of each run, Pallas kernels for 0% -> 0%
where the time goes in v1:
time: 286 us; the launch traced here: 283 us
  Pallas kernels  267 us (93%)
  local copies, waits for them, and re-layouts  15.3 us (5%)
    pallas_call x1, Pallas kernels, body(): pl.pallas_call(kernel, out_shape=(result, result), in_specs=[vmem] * 4 +...  267 us
    unnamed x8, local copies, waits for them, and re-layouts  9.75 us

profile of v1, /device:TPU:7, one launch (start us, length us, event | category | flops | bytes accessed | tf_op | source)
XLA Modules:
  0.0 282.6 jit_solution(4736936426669467976)
XLA Ops:
  0.6 1.4 copy.14.routes_one
  2.0 1.4 copy.15.probs_one
  3.4 1.4 copy.16.routes_two
  4.8 1.4 copy.17.probs_two
  6.2 0.0 copy-start
  6.2 4.0 %copy.12 = bf16[1,4096,192]{2,1,0:T(8,128)(2,1)} copy(bf16[1,4096,192]{1,2,0:T(8,128)(2,1)} %param.17) | data formatting | bytes 3145728 | tf_op args[7]
  10.1 0.0 copy-done
  10.2 2.4 copy.13
  12.6 266.6 %shard_map.113 = (bf16[128,4096]{1,0:T(8,128)(2,1)}, bf16[128,4096]{1,0:T(8,128)(2,1)}) custom-call(s32[128,1]{1,0:T(8,128)} %copy.14.routes_one, f32[128,1]{1,0:T(8,128)} %copy.15.probs_one, s32[128,1]{1,0:T(8,128)} %copy.16.routes_two, f32[128,1]{1,0:T(8,128)} %copy.17.probs_two, bf16[128,4096]{1,0:T(8,128)(2,1)} %bitcast.15, bf16[128,4096]{1,0:T(8,128)(2,1)} %bitcast.16, ...), custom_call_target="tpu_custom_call" | custom-call | tf_op jit(solution)/shard_map/pallas_call | solution.py:479
  279.2 0.0 copy-start.1
  279.2 2.4 copy.20
  281.6 0.0 copy-done.1
  281.6 1.0 copy.21
Async XLA Ops:
  6.2 4.0 %copy-start = (bf16[1,4096,192]{1,2,0:T(8,128)(2,1)S(1)}, bf16[1,4096,192]{1,2,0:T(8,128)(2,1)}, u32[]{:S(2)}) copy-start(bf16[1,4096,192]{1,2,0:T(8,128)(2,1)} %param.18) | copy-start | bytes 4718596
  279.2 2.4 copy-start.1

commit v2 on v1

v2 whole, which is shorter than its diff:
```python
import jax
import jax.numpy as jnp
from jax import lax
from jax.experimental import pallas as pl
from jax.experimental.pallas import tpu as pltpu
from jax.sharding import PartitionSpec as P

MESH = pl.DeviceIdType.MESH
F32 = jnp.float32
BF16 = jnp.bfloat16
NT = (((1,), (1,)), ((), ()))

TOK = 128
D = 4096
HID = 192
EXPERTS = 8
KB = 512
NK = D // KB
W = D + KB
BLK = 16
SRC = 32
HALF = SRC // 2
MAIN = HALF * BLK
EXTRA = HALF * 2
ROWS = MAIN + EXTRA
SECTIONS = 8

ONE, ACTS, GRADS = 0, 1, 2


def rows16(index):
    return pl.ds(pl.multiple_of(index * BLK, BLK), BLK)


def cols(index):
    return pl.ds(pl.multiple_of(index * KB, KB), KB)


def iota(shape, dim):
    return lax.broadcasted_iota(jnp.int32, shape, dim)


def onehot(mask):
    return jnp.where(mask, 1.0, 0.0).astype(BF16)


def column(row):
    eye = iota((TOK, TOK), 0) == iota((TOK, TOK), 1)
    return jnp.sum(jnp.where(eye, jnp.broadcast_to(row, (TOK, TOK)), 0.0), axis=1, keepdims=True)


def codes(expert_row):
    here, there = iota((TOK, TOK), 0), iota((TOK, TOK), 1)
    row = expert_row.astype(F32)
    col = column(row)
    same = jnp.where(col == row, 1.0, 0.0)
    slot_col = jnp.sum(jnp.where(there < here, same, 0.0), axis=1, keepdims=True)
    slot_row = jnp.sum(jnp.where(here < there, same, 0.0), axis=0, keepdims=True)

    def both(expert, slot):
        main = jnp.where(slot < BLK, expert * BLK + slot, -1.0)
        tail = jnp.where(slot < BLK, -1024.0, expert * BLK + slot - BLK)
        return main, tail

    return both(col, slot_col), both(row, slot_row)


def entry_own(z, q):
    return jnp.where(q == 0, jnp.minimum(z, 1), jnp.maximum(z, 2))


def entry_far(z, q):
    return jnp.where(q == 0, jnp.where(z == 0, 1, 0), jnp.where(z == 3, 2, 3))


def kernel(
    routes_one, probs_one, routes_two, probs_two, one_hbm, acts_hbm, grads_hbm, gate_hbm, up_hbm, down_hbm,
    out_one, out_two,
    held, wg, wu, wd, meta_out, meta_in, stage, recv, part, cx, px, home, acc, hid,
    load_sem, msend, mrecv, dsend, fsend, csend, rsem, xsend, xrecv, psend, precv, hsend, hrecv,
):
    p, j = lax.axis_index("pipe"), lax.axis_index("ep")
    x, z, c = j // 8, (j // 2) % 4, j % 2
    q = z // 2
    expert = j // 4
    other = x * 8 + z * 2 + (1 - c)
    pair = x * 8 + (q * 4 + 1 - z) * 2 + c
    after, before = lax.rem(p + 1, SECTIONS), lax.rem(p + SECTIONS - 1, SECTIONS)
    section = {ONE: after, ACTS: p, GRADS: before}

    def entry(d, source_z, pair_index):
        return entry_own(source_z, pair_index) if d == ACTS else entry_far(source_z, pair_index)

    loads = [
        pltpu.make_async_copy(src, dst, load_sem.at[i])
        for i, (src, dst) in enumerate(
            [
                (acts_hbm, held.at[ACTS]),
                (one_hbm, held.at[ONE]),
                (grads_hbm, held.at[GRADS]),
                (gate_hbm, wg),
                (up_hbm, wu),
                (down_hbm, wd),
            ]
        )
    ]
    for load in loads:
        load.start()

    barrier = pltpu.get_barrier_semaphore()

    def greet(n, carry):
        them = (n // 4) * 8 + (n % 4) * 2 + c
        pl.semaphore_signal(barrier, inc=1, device_id=(after, them), device_id_type=MESH)
        pl.semaphore_signal(barrier, inc=1, device_id=(before, them), device_id_type=MESH)

        @pl.when(them != j)
        def _():
            pl.semaphore_signal(barrier, inc=1, device_id=(p, them), device_id_type=MESH)

        return carry

    lax.fori_loop(0, 16, greet, 0)
    pl.semaphore_signal(barrier, inc=1, device_id=(p, other), device_id_type=MESH)

    (main_col_one, tail_col_one), (main_row_one, tail_row_one) = codes(routes_one[...])
    (main_col_two, tail_col_two), (main_row_two, tail_row_two) = codes(routes_two[...])
    meta_out[0, 0:1, :] = main_row_one
    meta_out[0, 1:2, :] = tail_row_one
    meta_out[0, 2:8, :] = jnp.zeros((6, TOK), F32)
    meta_out[1, 0:1, :] = main_row_two
    meta_out[1, 1:2, :] = tail_row_two
    meta_out[1, 2:3, :] = probs_two[...]
    meta_out[1, 3:8, :] = jnp.zeros((5, TOK), F32)

    pl.semaphore_wait(barrier, 48)

    metas = [
        pltpu.make_async_remote_copy(
            meta_out.at[i], meta_in.at[i], msend.at[i], mrecv.at[i], device_id=(to, j), device_id_type=MESH
        )
        for i, to in enumerate((before, after))
    ]
    for copy in metas:
        copy.start()

    def fill(d, main_row, tail_row, prob_row):
        row = iota((TOK, TOK), 0).astype(F32)
        here = row == main_row
        table = onehot(here)
        tail = jnp.zeros((TOK, KB), F32)
        tail_prob = jnp.zeros((TOK, 1), F32)
        if prob_row is not None:
            prob = jnp.sum(jnp.where(here, prob_row, 0.0), axis=1, keepdims=True)
        for k in range(NK):
            values = held[d, :, k * KB : (k + 1) * KB]
            got = jnp.dot(table, values, preferred_element_type=F32)
            there = row == tail_row + 2.0 * k
            tail = tail + jnp.dot(onehot(there), values, preferred_element_type=F32)
            if prob_row is not None:
                got = prob * got
                tail_prob = tail_prob + jnp.sum(jnp.where(there, prob_row, 0.0), axis=1, keepdims=True)
            stage[d, :, k * KB : (k + 1) * KB] = got.astype(BF16)
        if prob_row is not None:
            tail = tail_prob * tail
        stage[d, :, D:W] = tail.astype(BF16)

    def place(r, core, source_z):
        return r // 2, (r % 2) * 8 + core * 4 + source_z

    def source(i):
        return i // 4, jnp.where(q == 0, 3 - i % 4, i % 4)

    def launch(move, may_stay):
        target, src, dst, send_sem, sem, device = move

        def remote():
            pltpu.make_async_remote_copy(src, dst, send_sem, sem, device_id=device, device_id_type=MESH).start()

        if not may_stay:
            remote()
            return
        pl.when(target != j)(remote)

        @pl.when(target == j)
        def _():
            pltpu.make_async_copy(src, dst, sem).start()

    def sent(move, may_stay, when=True):
        target, src, dst, send_sem, sem, device = move

        def wait():
            pltpu.make_async_remote_copy(src, dst, send_sem, sem, device_id=device, device_id_type=MESH).wait_send()

        if may_stay:
            pl.when(jnp.logical_and(when, target != j))(wait)
        else:
            wait()

    def dispatch(d, i):
        r = i // 2
        e = lax.rem(x + r, 4) * 2 + i % 2
        target = (e // 2) * 8 + entry(d, z, e % 2) * 2 + c
        h, b = place(r, c, z)
        sem = rsem.at[d, h * HALF + b]
        src, dst = stage.at[d, rows16(e)], recv.at[d, h, rows16(b)]
        return target, src, dst, dsend.at[d, i], sem, (section[d], target)

    def send(d, low, high):
        def step(i, carry):
            launch(dispatch(d, i), d == ACTS)
            return carry

        lax.fori_loop(low, high, step, 0)

    def arrived(d, h, b):
        ref = recv.at[d, h, rows16(b)]
        pltpu.make_async_copy(ref, ref, rsem.at[d, h * HALF + b]).wait()

    def onward(d, i, to, sem):
        r, source_z = source(i)
        h, b = place(r, c, source_z)
        ref = recv.at[d, h, rows16(b)]
        return pltpu.make_async_remote_copy(
            ref, ref, sem.at[d, i], rsem.at[d, h * HALF + b], device_id=(p, to), device_id_type=MESH
        )

    def forward(d, half, direct):
        def step(i, carry):
            r, source_z = source(i)
            enters = entry(d, source_z, q) == z

            @pl.when(enters if direct else jnp.logical_not(enters))
            def _():
                h, b = place(r, c, source_z)
                arrived(d, h, b)
                if direct:
                    onward(d, i, pair, fsend).start()
                onward(d, i, other, csend).start()

            return carry

        lax.fori_loop(half * 8, half * 8 + 8, step, 0)

    def from_core(d, half):
        def step(i, carry):
            r, source_z = source(i)
            h, b = place(r, 1 - c, source_z)
            arrived(d, h, b)
            return carry

        lax.fori_loop(half * 8, half * 8 + 8, step, 0)

    def unfold(d, h):
        row, col = iota((EXTRA, MAIN), 0), iota((EXTRA, MAIN), 1)
        base = (row // 2) * BLK + row % 2
        tail = recv[d, h, 0:MAIN, D:W]
        for k in range(NK):
            pick = onehot(col == base + 2 * k)
            recv[d, h, MAIN:ROWS, k * KB : (k + 1) * KB] = jnp.dot(pick, tail, preferred_element_type=F32).astype(BF16)

    def fold(m, h):
        row, col = iota((MAIN, EXTRA), 0), iota((MAIN, EXTRA), 1)
        base = (col // 2) * BLK + col % 2
        tail = jnp.zeros((MAIN, KB), F32)
        for k in range(NK):
            pick = onehot(row == base + 2 * k)
            tail = tail + jnp.dot(pick, part[m, h, MAIN:ROWS, k * KB : (k + 1) * KB], preferred_element_type=F32)
        part[m, h, 0:MAIN, D:W] = tail.astype(BF16)

    def gate_up(d, h):
        unfold(d, h)
        acc[h, 0:2] = jnp.zeros((2, ROWS, HID), F32)

        def step(k, carry):
            values = recv[d, h, :, cols(k)]
            acc[h, 0] += lax.dot_general(values, wg[:, cols(k)], NT, preferred_element_type=F32)
            acc[h, 1] += lax.dot_general(values, wu[:, cols(k)], NT, preferred_element_type=F32)
            return carry

        lax.fori_loop(0, NK, step, 0)

    def forward_compute(h):
        gate_up(ONE, h)
        gate = acc[h, 0]
        hid[0] = (gate * jax.nn.sigmoid(gate) * acc[h, 1]).astype(BF16)

        def step(k, carry):
            part[0, h, :, cols(k)] = jnp.dot(hid[0], wd[:, cols(k)], preferred_element_type=F32).astype(BF16)
            return carry

        lax.fori_loop(0, NK, step, 0)
        fold(0, h)

    def backward_compute(h):
        unfold(GRADS, h)
        acc[h, 2] = jnp.zeros((ROWS, HID), F32)

        def down(k, carry):
            acc[h, 2] += lax.dot_general(recv[GRADS, h, :, cols(k)], wd[:, cols(k)], NT, preferred_element_type=F32)
            return carry

        lax.fori_loop(0, NK, down, 0)
        gate = acc[h, 0]
        sig = jax.nn.sigmoid(gate)
        slope = acc[h, 2] * sig
        hid[0] = (slope * acc[h, 1] * (1.0 + gate * (1.0 - sig))).astype(BF16)
        hid[1] = (slope * gate).astype(BF16)

        def step(k, carry):
            total = jnp.dot(hid[0], wg[:, cols(k)], preferred_element_type=F32)
            total = total + jnp.dot(hid[1], wu[:, cols(k)], preferred_element_type=F32)
            part[1, h, :, cols(k)] = total.astype(BF16)
            return carry

        lax.fori_loop(0, NK, step, 0)
        fold(1, h)

    def to_core(m, r):
        return pltpu.make_async_remote_copy(
            part.at[m, r // 2, pl.ds(pl.multiple_of(((r % 2) * 8 + (1 - c) * 4) * BLK, 64), 64)],
            cx.at[m, r],
            xsend.at[m, r],
            xrecv.at[m, r],
            device_id=(p, other),
            device_id_type=MESH,
        )

    def add_into(m, i, extra):
        r, source_z = source(i)
        h, b = place(r, c, source_z)
        part[m, h, rows16(b), :] = (part[m, h, rows16(b), :].astype(F32) + extra.astype(F32)).astype(BF16)

    def to_pair(m, i):
        r, source_z = source(i)
        h, b = place(r, c, source_z)
        return pltpu.make_async_remote_copy(
            part.at[m, h, rows16(b)],
            px.at[m, i],
            psend.at[m, i],
            precv.at[m, i],
            device_id=(p, pair),
            device_id_type=MESH,
        )

    def to_home(m, i):
        r, source_z = source(i)
        h, b = place(r, c, source_z)
        target = lax.rem(x + 4 - r, 4) * 8 + source_z * 2 + c
        src, dst, sem = part.at[m, h, rows16(b)], home.at[m, rows16(expert)], hrecv.at[m, expert]
        return target, src, dst, hsend.at[m, i], sem, (p, target)

    def leaves_here(i):
        return entry_own(source(i)[1], q) == z

    def return_first(m, half):
        for r in (half * 2, half * 2 + 1):
            pltpu.make_async_copy(cx.at[m, r], cx.at[m, r], xrecv.at[m, r]).wait()

            def step(i, carry):
                add_into(m, i, cx[m, r, rows16(source(i)[1]), :])

                @pl.when(jnp.logical_not(leaves_here(i)))
                def _():
                    to_pair(m, i).start()

                return carry

            lax.fori_loop(r * 4, r * 4 + 4, step, 0)

    def return_second(m, half):
        def step(i, carry):
            @pl.when(leaves_here(i))
            def _():
                pltpu.make_async_copy(px.at[m, i], px.at[m, i], precv.at[m, i]).wait()
                add_into(m, i, px[m, i])
                launch(to_home(m, i), True)

            return carry

        lax.fori_loop(half * 8, half * 8 + 8, step, 0)

    def collect(m, main_col, tail_col, prob_col, out):
        def step(e, carry):
            pltpu.make_async_copy(home.at[m, rows16(e)], home.at[m, rows16(e)], hrecv.at[m, e]).wait()
            return carry

        lax.fori_loop(0, EXPERTS, step, 0)
        row = iota((TOK, TOK), 1).astype(F32)
        table = onehot(row == main_col)
        tail = home[m, :, D:W]
        for k in range(NK):
            got = jnp.dot(table, home[m, :, k * KB : (k + 1) * KB], preferred_element_type=F32)
            got = got + jnp.dot(onehot(row == tail_col + 2.0 * k), tail, preferred_element_type=F32)
            if prob_col is not None:
                got = prob_col * got
            out[:, k * KB : (k + 1) * KB] = got.astype(BF16)

    loads[0].wait()
    fill(ACTS, main_row_two, tail_row_two, None)
    send(ACTS, 0, 8)
    loads[1].wait()
    metas[0].wait_recv()
    fill(ONE, meta_in[0, 0:1, :], meta_in[0, 1:2, :], None)
    send(ONE, 0, 8)
    forward(ACTS, 0, True)
    forward(ACTS, 1, True)
    forward(ONE, 0, True)
    forward(ONE, 1, True)
    loads[2].wait()
    metas[1].wait_recv()
    fill(GRADS, meta_in[1, 0:1, :], meta_in[1, 1:2, :], meta_in[1, 2:3, :])
    send(GRADS, 0, 8)
    for load in loads[3:]:
        load.wait()
    forward(ONE, 0, False)
    from_core(ONE, 0)
    forward_compute(0)
    to_core(0, 0).start()
    to_core(0, 1).start()
    forward(ONE, 1, False)
    return_first(0, 0)
    from_core(ONE, 1)
    forward_compute(1)
    to_core(0, 2).start()
    to_core(0, 3).start()
    forward(GRADS, 0, True)
    return_first(0, 1)
    forward(ACTS, 0, False)
    forward(ACTS, 1, False)
    from_core(ACTS, 0)
    gate_up(ACTS, 0)
    from_core(ACTS, 1)
    gate_up(ACTS, 1)
    forward(GRADS, 1, True)
    return_second(0, 0)
    forward(GRADS, 0, False)
    return_second(0, 1)
    from_core(GRADS, 0)
    backward_compute(0)
    to_core(1, 0).start()
    to_core(1, 1).start()
    forward(GRADS, 1, False)
    return_first(1, 0)
    from_core(GRADS, 1)
    backward_compute(1)
    to_core(1, 2).start()
    to_core(1, 3).start()
    return_first(1, 1)
    collect(0, main_col_one, tail_col_one, column(probs_one[...]), out_one)
    return_second(1, 0)
    return_second(1, 1)
    collect(1, main_col_two, tail_col_two, None, out_two)

    for copy in metas:
        copy.wait_send()

    for d in (ACTS, ONE, GRADS):

        def injected(i, carry):
            sent(dispatch(d, i), d == ACTS)
            return carry

        lax.fori_loop(0, EXPERTS, injected, 0)

        def passed(i, carry):
            @pl.when(entry(d, source(i)[1], q) == z)
            def _():
                onward(d, i, pair, fsend).wait_send()

            onward(d, i, other, csend).wait_send()
            return carry

        lax.fori_loop(0, 16, passed, 0)

    for m in range(2):
        for r in range(4):
            to_core(m, r).wait_send()

        def returned(i, carry):
            leaves = leaves_here(i)

            @pl.when(jnp.logical_not(leaves))
            def _():
                to_pair(m, i).wait_send()

            sent(to_home(m, i), True, leaves)
            return carry

        lax.fori_loop(0, 16, returned, 0)


def body(
    first_acts,
    first_routes,
    first_probs,
    second_acts,
    second_grads,
    second_routes,
    second_probs,
    gate_weight,
    up_weight,
    down_weight,
):
    vmem = pl.BlockSpec(memory_space=pltpu.VMEM)
    hbm = pl.BlockSpec(memory_space=pl.ANY)
    dma = pltpu.SemaphoreType.DMA
    result = jax.ShapeDtypeStruct((TOK, D), BF16)
    first_out, input_grads = pl.pallas_call(
        kernel,
        out_shape=(result, result),
        in_specs=[vmem] * 4 + [hbm] * 6,
        out_specs=(vmem, vmem),
        scratch_shapes=[
            pltpu.VMEM((3, TOK, D), BF16),
            pltpu.VMEM((HID, D), BF16),
            pltpu.VMEM((HID, D), BF16),
            pltpu.VMEM((HID, D), BF16),
            pltpu.VMEM((2, 8, TOK), F32),
            pltpu.VMEM((2, 8, TOK), F32),
            pltpu.VMEM((3, EXPERTS * BLK, W), BF16),
            pltpu.VMEM((3, 2, ROWS, W), BF16),
            pltpu.VMEM((2, 2, ROWS, W), BF16),
            pltpu.VMEM((2, 4, 4 * BLK, W), BF16),
            pltpu.VMEM((2, 16, BLK, W), BF16),
            pltpu.VMEM((2, EXPERTS * BLK, W), BF16),
            pltpu.VMEM((2, 3, ROWS, HID), F32),
            pltpu.VMEM((2, ROWS, HID), BF16),
            dma((6,)),
            dma((2,)),
            dma((2,)),
            dma((3, EXPERTS)),
            dma((3, 16)),
            dma((3, 16)),
            dma((3, SRC)),
            dma((2, 4)),
            dma((2, 4)),
            dma((2, 16)),
            dma((2, 16)),
            dma((2, 16)),
            dma((2, EXPERTS)),
        ],
        compiler_params=pltpu.CompilerParams(
            collective_id=0, has_side_effects=True, vmem_limit_bytes=63 * 1024 * 1024
        ),
    )(
        first_routes.reshape(1, TOK),
        first_probs.reshape(1, TOK),
        second_routes.reshape(1, TOK),
        second_probs.reshape(1, TOK),
        first_acts[0],
        second_acts[0],
        second_grads[0],
        gate_weight[0].T,
        up_weight[0].T,
        down_weight[0],
    )
    return (first_out[None], input_grads[None])


def solution(mesh):
    in_specs = (
        P("pipe", "ep", None),
        P("pipe", "ep", None),
        P("pipe", "ep", None),
        P("pipe", "ep", None),
        P("pipe", "ep", None),
        P("pipe", "ep", None),
        P("pipe", "ep", None),
        P("pipe", None, "ep"),
        P("pipe", None, "ep"),
        P("pipe", "ep", None),
    )
    out_specs = (P("pipe", "ep", None), P("pipe", "ep", None))
    return jax.shard_map(body, mesh=mesh, in_specs=in_specs, out_specs=out_specs, check_vma=False)
```

time: 286 us -> 244 us (0.85)
  the two profiles are of different devices: /device:TPU:7 before, /device:TPU:200 now
where the time goes in v2:
time: 244 us
  Pallas kernels  240 us (98%)
  local copies, waits for them, and re-layouts  3.35 us (1%)
    pallas_call x1, Pallas kernels, body(): pl.pallas_call(kernel, out_shape=(result, result), in_specs=[vmem] * 4 +...  240 us

profile of v2, /device:TPU:200, one launch (start us, length us, event | category | flops | bytes accessed | tf_op | source)
XLA Modules:
  0.0 243.7 jit_solution(17370039261656026899)
XLA Ops:
  0.6 239.7 %shard_map.113 = (bf16[128,4096]{1,0:T(8,128)(2,1)}, bf16[128,4096]{1,0:T(8,128)(2,1)}) custom-call(s32[1,128]{1,0:T(1,128)} %bitcast.24, f32[1,128]{1,0:T(1,128)} %bitcast.25, s32[1,128]{1,0:T(1,128)} %bitcast.26, f32[1,128]{1,0:T(1,128)} %bitcast.27, bf16[128,4096]{1,0:T(8,128)(2,1)} %bitcast.19, bf16[128,4096]{1,0:T(8,128)(2,1)} %bitcast.20, ...), custom_call_target="tpu_custom_call" | custom-call | tf_op jit(solution)/shard_map/pallas_call | solution.py:509
  240.3 0.0 copy-start
  240.3 2.4 copy.14
  242.7 0.0 copy-done
  242.7 1.0 copy.15
Async XLA Ops:
  240.3 2.4 copy-start

commit v3 on v2

v3 whole, which is shorter than its diff:
```python
import jax
import jax.numpy as jnp
from jax import lax
from jax.experimental import pallas as pl
from jax.experimental.pallas import tpu as pltpu
from jax.sharding import PartitionSpec as P

MESH = pl.DeviceIdType.MESH
F32 = jnp.float32
BF16 = jnp.bfloat16
NT = (((1,), (1,)), ((), ()))

TOK = 128
D = 4096
HID = 192
EXPERTS = 8
KB = 512
NK = D // KB
W = D + KB
BLK = 16
SRC = 32
SPLIT = 4
PIECE = HID // SPLIT
PIECES = 3 * SPLIT
HALF = SRC // 2
MAIN = HALF * BLK
EXTRA = HALF * 2
ROWS = MAIN + EXTRA
SECTIONS = 8

ONE, ACTS, GRADS = 0, 1, 2


def rows16(index):
    return pl.ds(pl.multiple_of(index * BLK, BLK), BLK)


def cols(index):
    return pl.ds(pl.multiple_of(index * KB, KB), KB)


def iota(shape, dim):
    return lax.broadcasted_iota(jnp.int32, shape, dim)


def onehot(mask):
    return jnp.where(mask, 1.0, 0.0).astype(BF16)


def column(row):
    eye = iota((TOK, TOK), 0) == iota((TOK, TOK), 1)
    return jnp.sum(jnp.where(eye, jnp.broadcast_to(row, (TOK, TOK)), 0.0), axis=1, keepdims=True)


def codes(expert_row):
    here, there = iota((TOK, TOK), 0), iota((TOK, TOK), 1)
    row = expert_row.astype(F32)
    col = column(row)
    same = jnp.where(col == row, 1.0, 0.0)
    slot_col = jnp.sum(jnp.where(there < here, same, 0.0), axis=1, keepdims=True)
    slot_row = jnp.sum(jnp.where(here < there, same, 0.0), axis=0, keepdims=True)

    def both(expert, slot):
        main = jnp.where(slot < BLK, expert * BLK + slot, -1.0)
        tail = jnp.where(slot < BLK, -1024.0, expert * BLK + slot - BLK)
        return main, tail

    return both(col, slot_col), both(row, slot_row)


def flip(z, k):
    return (z % 2 + k % 2) % 2 + 2 * ((z // 2 + k // 2) % 2)


def kernel(
    routes_one, probs_one, routes_two, probs_two, one_hbm, acts_hbm, grads_hbm, gate_hbm, up_hbm, down_hbm,
    out_one, out_two,
    held, held_w, meta_out, meta_in, stage, recv, part, cx, px, home, acc, hid, relay,
    load_sem, msend, mrecv, dsend, fsend, csend, rsem, xsend, xrecv, psend, precv, hsend, hrecv,
    wsend, wrecv, relay_recv, out_sem,
):
    p, j = lax.axis_index("pipe"), lax.axis_index("ep")
    x, z, c = j // 8, (j // 2) % 4, j % 2
    columns = x // 2
    flipped_x, flipped_z = flip(x, 1), flip(z, 1)
    expert = (columns * 2 + z % 2) * 2 + z // 2
    other = x * 8 + z * 2 + (1 - c)
    pair = flipped_x * 8 + z * 2 + c
    even = x % 2 == z % 2
    relays = jnp.logical_and(c == 1, even)
    round_x, round_z = jnp.where(even, flipped_x, x), jnp.where(even, z, flipped_z)
    beside = flipped_x * 8 + z * 2 + 1
    beyond = x * 8 + flipped_z * 2 + 1
    after, before = lax.rem(p + 1, SECTIONS), lax.rem(p + SECTIONS - 1, SECTIONS)
    section = {ONE: after, ACTS: p, GRADS: before}

    loads = [
        pltpu.make_async_copy(src, held.at[d], load_sem.at[d])
        for d, src in ((ACTS, acts_hbm), (ONE, one_hbm), (GRADS, grads_hbm))
    ]
    for load in loads:
        load.start()

    weights = (gate_hbm, up_hbm, down_hbm)

    def slot(i, n):
        return held_w.at[i, pl.ds(n * PIECE, PIECE)]

    def keep_weights():
        for i in range(3):
            for n in range(SPLIT):
                src = weights[i].at[pl.ds(n * PIECE, PIECE)]
                pl.when(relays)(pltpu.make_async_copy(src, slot(i, n), wrecv.at[i * SPLIT + n]).start)

    def give_weight(i, n):
        part_of, t = pl.ds(pl.multiple_of(n * PIECE, BLK), PIECE), i * SPLIT + n
        src = weights[i].at[part_of]

        @pl.when(c == 0)
        def _():
            pltpu.make_async_remote_copy(
                src, held_w.at[i, part_of], wsend.at[t], wrecv.at[t],
                device_id=(p, round_x * 8 + round_z * 2), device_id_type=MESH,
            ).start()

        @pl.when(jnp.logical_and(c == 1, jnp.logical_not(even)))
        def _():
            pltpu.make_async_remote_copy(
                src, relay.at[t], wsend.at[t], relay_recv.at[t], device_id=(p, beside), device_id_type=MESH
            ).start()

    def give_all(i):
        def step(n, carry):
            give_weight(i, n)
            return carry

        lax.fori_loop(0, SPLIT, step, 0)

    def relay_weight(t):
        @pl.when(relays)
        def _():
            pltpu.make_async_copy(relay.at[t], relay.at[t], relay_recv.at[t]).wait()
            pltpu.make_async_remote_copy(
                relay.at[t],
                held_w.at[t // SPLIT, pl.ds(pl.multiple_of((t % SPLIT) * PIECE, BLK), PIECE)],
                wsend.at[t],
                wrecv.at[t],
                device_id=(p, beyond),
                device_id_type=MESH,
            ).start()

    def weights_here():
        for i in range(3):
            for n in range(SPLIT):
                pltpu.make_async_copy(slot(i, n), slot(i, n), wrecv.at[i * SPLIT + n]).wait()

    barrier = pltpu.get_barrier_semaphore()

    def greet(n, carry):
        them = (n // 4) * 8 + (n % 4) * 2 + c
        pl.semaphore_signal(barrier, inc=1, device_id=(after, them), device_id_type=MESH)
        pl.semaphore_signal(barrier, inc=1, device_id=(before, them), device_id_type=MESH)

        @pl.when(them != j)
        def _():
            pl.semaphore_signal(barrier, inc=1, device_id=(p, them), device_id_type=MESH)

        return carry

    lax.fori_loop(0, 16, greet, 0)
    pl.semaphore_signal(barrier, inc=1, device_id=(p, other), device_id_type=MESH)

    (main_col_one, tail_col_one), (main_row_one, tail_row_one) = codes(routes_one[...])
    (main_col_two, tail_col_two), (main_row_two, tail_row_two) = codes(routes_two[...])
    meta_out[0, 0:1, :] = main_row_one
    meta_out[0, 1:2, :] = tail_row_one
    meta_out[0, 2:8, :] = jnp.zeros((6, TOK), F32)
    meta_out[1, 0:1, :] = main_row_two
    meta_out[1, 1:2, :] = tail_row_two
    meta_out[1, 2:3, :] = probs_two[...]
    meta_out[1, 3:8, :] = jnp.zeros((5, TOK), F32)

    pl.semaphore_wait(barrier, 48)

    metas = [
        pltpu.make_async_remote_copy(
            meta_out.at[i], meta_in.at[i], msend.at[i], mrecv.at[i], device_id=(to, j), device_id_type=MESH
        )
        for i, to in enumerate((before, after))
    ]
    for copy in metas:
        copy.start()

    def fill(d, main_row, tail_row, prob_row):
        row = iota((TOK, TOK), 0).astype(F32)
        here = row == main_row
        table = onehot(here)
        tail = jnp.zeros((TOK, KB), F32)
        tail_prob = jnp.zeros((TOK, 1), F32)
        if prob_row is not None:
            prob = jnp.sum(jnp.where(here, prob_row, 0.0), axis=1, keepdims=True)
        for k in range(NK):
            values = held[d, :, k * KB : (k + 1) * KB]
            got = jnp.dot(table, values, preferred_element_type=F32)
            there = row == tail_row + 2.0 * k
            tail = tail + jnp.dot(onehot(there), values, preferred_element_type=F32)
            if prob_row is not None:
                got = prob * got
                tail_prob = tail_prob + jnp.sum(jnp.where(there, prob_row, 0.0), axis=1, keepdims=True)
            stage[d, :, k * KB : (k + 1) * KB] = got.astype(BF16)
        if prob_row is not None:
            tail = tail_prob * tail
        stage[d, :, D:W] = tail.astype(BF16)

    def place(parity, core, source_z):
        return parity * 8 + core * 4 + source_z

    def enters(half):
        return (x + half) % 2

    def launch(move, may_stay):
        target, src, dst, send_sem, sem, device = move

        def remote():
            pltpu.make_async_remote_copy(src, dst, send_sem, sem, device_id=device, device_id_type=MESH).start()

        if not may_stay:
            remote()
            return
        pl.when(target != j)(remote)

        @pl.when(target == j)
        def _():
            pltpu.make_async_copy(src, dst, sem).start()

    def sent(move, may_stay):
        target, src, dst, send_sem, sem, device = move

        def wait():
            pltpu.make_async_remote_copy(src, dst, send_sem, sem, device_id=device, device_id_type=MESH).wait_send()

        if may_stay:
            pl.when(target != j)(wait)
        else:
            wait()

    def dispatch(d, i):
        half = i // 4
        to_z = flip(z, i % 4 if d == ACTS else 3 - i % 4)
        to_columns = jnp.where(half == 0, columns, 1 - columns)
        target = jnp.where(half == 0, x, 3 - x) * 8 + to_z * 2 + c
        e = (to_columns * 2 + to_z % 2) * 2 + to_z // 2
        b = place(x % 2, c, z)
        sem = rsem.at[d, half * HALF + b]
        src, dst = stage.at[d, rows16(e)], recv.at[d, half, rows16(b)]
        return target, src, dst, dsend.at[d, i], sem, (section[d], target)

    def send(d, low, high):
        def step(i, carry):
            launch(dispatch(d, i), d == ACTS)
            return carry

        lax.fori_loop(low, high, step, 0)

    def arrived(d, h, b):
        ref = recv.at[d, h, rows16(b)]
        pltpu.make_async_copy(ref, ref, rsem.at[d, h * HALF + b]).wait()

    def onward(d, half, b, to, sem):
        ref = recv.at[d, half, rows16(b)]
        return pltpu.make_async_remote_copy(
            ref, ref, sem, rsem.at[d, half * HALF + b], device_id=(p, to), device_id_type=MESH
        )

    def to_pair_sem(d, half, source_z):
        return fsend.at[d, half * 4 + source_z]

    def to_core_sem(d, half, parity, source_z):
        return csend.at[d, half * 8 + parity * 4 + source_z]

    def forward(d, half, direct, give=None, relay_of=None):
        parity = enters(half) if direct else 1 - enters(half)

        def step(k, carry):
            source_z = flip(z, k if d == ACTS else 3 - k)
            b = place(parity, c, source_z)
            arrived(d, half, b)
            if direct:
                onward(d, half, b, pair, to_pair_sem(d, half, source_z)).start()
            onward(d, half, b, other, to_core_sem(d, half, parity, source_z)).start()
            if give is not None:
                give_weight(give, k)
            if relay_of is not None:
                relay_weight(relay_of * SPLIT + k)
            return carry

        lax.fori_loop(0, 4, step, 0)

    def from_core(d, half):
        def step(k, carry):
            arrived(d, half, place(k // 4, 1 - c, k % 4))
            return carry

        lax.fori_loop(0, 8, step, 0)

    def unfold(d, h):
        row, col = iota((EXTRA, MAIN), 0), iota((EXTRA, MAIN), 1)
        base = (row // 2) * BLK + row % 2
        tail = recv[d, h, 0:MAIN, D:W]
        for k in range(NK):
            pick = onehot(col == base + 2 * k)
            recv[d, h, MAIN:ROWS, k * KB : (k + 1) * KB] = jnp.dot(pick, tail, preferred_element_type=F32).astype(BF16)

    def fold(m, h):
        row, col = iota((MAIN, EXTRA), 0), iota((MAIN, EXTRA), 1)
        base = (col // 2) * BLK + col % 2
        tail = jnp.zeros((MAIN, KB), F32)
        for k in range(NK):
            pick = onehot(row == base + 2 * k)
            tail = tail + jnp.dot(pick, part[m, h, MAIN:ROWS, k * KB : (k + 1) * KB], preferred_element_type=F32)
        part[m, h, 0:MAIN, D:W] = tail.astype(BF16)

    def gate_up(d, h):
        unfold(d, h)
        acc[h, 0:2] = jnp.zeros((2, ROWS, HID), F32)

        def step(k, carry):
            values = recv[d, h, :, cols(k)]
            acc[h, 0] += lax.dot_general(values, held_w[0, :, cols(k)], NT, preferred_element_type=F32)
            acc[h, 1] += lax.dot_general(values, held_w[1, :, cols(k)], NT, preferred_element_type=F32)
            return carry

        lax.fori_loop(0, NK, step, 0)

    def forward_compute(h):
        gate_up(ONE, h)
        gate = acc[h, 0]
        hid[0] = (gate * jax.nn.sigmoid(gate) * acc[h, 1]).astype(BF16)

        def step(k, carry):
            part[0, h, :, cols(k)] = jnp.dot(hid[0], held_w[2, :, cols(k)], preferred_element_type=F32).astype(BF16)
            return carry

        lax.fori_loop(0, NK, step, 0)
        fold(0, h)

    def backward_hidden(h):
        unfold(GRADS, h)
        acc[h, 2] = jnp.zeros((ROWS, HID), F32)

        def down(k, carry):
            acc[h, 2] += lax.dot_general(recv[GRADS, h, :, cols(k)], held_w[2, :, cols(k)], NT, preferred_element_type=F32)
            return carry

        lax.fori_loop(0, NK, down, 0)
        gate = acc[h, 0]
        sig = jax.nn.sigmoid(gate)
        slope = acc[h, 2] * sig
        hid[0] = (slope * acc[h, 1] * (1.0 + gate * (1.0 - sig))).astype(BF16)
        hid[1] = (slope * gate).astype(BF16)

    def backward_rows(h):
        def step(k, carry):
            total = jnp.dot(hid[0], held_w[0, :, cols(k)], preferred_element_type=F32)
            total = total + jnp.dot(hid[1], held_w[1, :, cols(k)], preferred_element_type=F32)
            part[1, h, :, cols(k)] = total.astype(BF16)
            return carry

        lax.fori_loop(0, NK, step, 0)
        fold(1, h)

    def to_core(m, half, parity):
        n = half * 2 + parity
        return pltpu.make_async_remote_copy(
            part.at[m, half, pl.ds(pl.multiple_of(place(parity, 1 - c, 0) * BLK, 64), 64)],
            cx.at[m, n],
            xsend.at[m, n],
            xrecv.at[m, n],
            device_id=(p, other),
            device_id_type=MESH,
        )

    def exchange(m, half):
        to_core(m, half, 1 - enters(half)).start()
        to_core(m, half, enters(half)).start()

    def add_into(m, half, b, extra):
        mine = part[m, half, rows16(b), :]
        part[m, half, rows16(b), :] = (mine.astype(F32) + extra.astype(F32)).astype(BF16)

    def to_pair(m, half, source_z):
        n = half * 4 + source_z
        return pltpu.make_async_remote_copy(
            part.at[m, half, rows16(place(1 - enters(half), c, source_z))],
            px.at[m, n],
            psend.at[m, n],
            precv.at[m, n],
            device_id=(p, pair),
            device_id_type=MESH,
        )

    def to_home(m, half, source_z):
        b = place(enters(half), c, source_z)
        target = (x if half == 0 else 3 - x) * 8 + source_z * 2 + c
        src, dst, sem = part.at[m, half, rows16(b)], home.at[m, rows16(expert)], hrecv.at[m, expert]
        return target, src, dst, hsend.at[m, half * 4 + source_z], sem, (p, target)

    def return_first(m, half):
        for parity, leaves in ((1 - enters(half), False), (enters(half), True)):
            n = half * 2 + parity
            pltpu.make_async_copy(cx.at[m, n], cx.at[m, n], xrecv.at[m, n]).wait()

            def step(k, carry):
                source_z = flip(z, 3 - k)
                add_into(m, half, place(parity, c, source_z), cx[m, n, rows16(source_z), :])
                if not leaves:
                    to_pair(m, half, source_z).start()
                return carry

            lax.fori_loop(0, 4, step, 0)

    def return_second(m, half):
        def step(k, carry):
            source_z = flip(z, 3 - k)
            n = half * 4 + source_z
            pltpu.make_async_copy(px.at[m, n], px.at[m, n], precv.at[m, n]).wait()
            add_into(m, half, place(enters(half), c, source_z), px[m, n])
            launch(to_home(m, half, source_z), half == 0)
            return carry

        lax.fori_loop(0, 4, step, 0)

    def drain_dispatch(d):
        def injected(i, carry):
            sent(dispatch(d, i), d == ACTS)
            return carry

        lax.fori_loop(0, EXPERTS, injected, 0)
        for half in range(2):

            def passed(k, carry):
                onward(d, half, place(enters(half), c, k), pair, to_pair_sem(d, half, k)).wait_send()
                for parity in range(2):
                    onward(d, half, place(parity, c, k), other, to_core_sem(d, half, parity, k)).wait_send()
                return carry

            lax.fori_loop(0, 4, passed, 0)

    def drain_return(m):
        for half in range(2):
            to_core(m, half, 0).wait_send()
            to_core(m, half, 1).wait_send()

            def returned(k, carry):
                to_pair(m, half, k).wait_send()
                sent(to_home(m, half, k), half == 0)
                return carry

            lax.fori_loop(0, 4, returned, 0)

    def drain_weights():
        def gone(t, carry):
            pltpu.make_async_remote_copy(
                relay.at[t], relay.at[t], wsend.at[t], wrecv.at[t], device_id=(p, beside), device_id_type=MESH
            ).wait_send()
            return carry

        lax.fori_loop(0, PIECES, gone, 0)

    def result(m, n, out):
        part_of = pl.ds(n * (D // 2), D // 2)
        return pltpu.make_async_copy(held.at[m, :, part_of], out.at[:, part_of], out_sem.at[m, n])

    def collect(m, main_col, tail_col, prob_col, out):
        def step(e, carry):
            pltpu.make_async_copy(home.at[m, rows16(e)], home.at[m, rows16(e)], hrecv.at[m, e]).wait()
            return carry

        lax.fori_loop(0, EXPERTS, step, 0)
        row = iota((TOK, TOK), 1).astype(F32)
        table = onehot(row == main_col)
        tail = home[m, :, D:W]
        for k in range(NK):
            got = jnp.dot(table, home[m, :, k * KB : (k + 1) * KB], preferred_element_type=F32)
            got = got + jnp.dot(onehot(row == tail_col + 2.0 * k), tail, preferred_element_type=F32)
            if prob_col is not None:
                got = prob_col * got
            held[m, :, k * KB : (k + 1) * KB] = got.astype(BF16)
            if k % 4 == 3:
                result(m, k // 4, out).start()

    loads[0].wait()
    fill(ACTS, main_row_two, tail_row_two, None)
    send(ACTS, 0, 8)
    keep_weights()
    loads[1].wait()
    metas[0].wait_recv()
    fill(ONE, meta_in[0, 0:1, :], meta_in[0, 1:2, :], None)
    send(ONE, 0, 8)
    give_all(0)
    give_all(1)
    give_all(2)
    forward(ACTS, 0, True, None, None)
    forward(ACTS, 1, True, None, 0)
    forward(ONE, 0, True, None, 1)
    forward(ONE, 1, True, None, 2)
    loads[2].wait()
    metas[1].wait_recv()
    fill(GRADS, meta_in[1, 0:1, :], meta_in[1, 1:2, :], meta_in[1, 2:3, :])
    send(GRADS, 0, 8)
    forward(ONE, 0, False)
    from_core(ONE, 0)
    forward(ONE, 1, False)
    forward(ACTS, 0, False)
    forward(ACTS, 1, False)
    forward(GRADS, 0, True)
    weights_here()
    forward_compute(0)
    exchange(0, 0)
    forward(GRADS, 1, True)
    from_core(ONE, 1)
    forward_compute(1)
    exchange(0, 1)
    return_first(0, 0)
    return_first(0, 1)
    from_core(ACTS, 0)
    forward(GRADS, 0, False)
    gate_up(ACTS, 0)
    from_core(ACTS, 1)
    forward(GRADS, 1, False)
    gate_up(ACTS, 1)
    from_core(GRADS, 0)
    backward_hidden(0)
    backward_rows(0)
    exchange(1, 0)
    return_second(0, 0)
    from_core(GRADS, 1)
    backward_hidden(1)
    return_first(1, 0)
    backward_rows(1)
    exchange(1, 1)
    return_second(0, 1)
    return_first(1, 1)
    return_second(1, 0)
    drain_dispatch(ACTS)
    drain_dispatch(ONE)
    drain_dispatch(GRADS)
    drain_weights()
    for copy in metas:
        copy.wait_send()
    return_second(1, 1)
    drain_return(0)
    collect(0, main_col_one, tail_col_one, column(probs_one[...]), out_one)
    collect(1, main_col_two, tail_col_two, None, out_two)
    drain_return(1)
    for n in range(2):
        result(0, n, out_one).wait()
        result(1, n, out_two).wait()


def body(
    first_acts,
    first_routes,
    first_probs,
    second_acts,
    second_grads,
    second_routes,
    second_probs,
    gate_weight,
    up_weight,
    down_weight,
):
    vmem = pl.BlockSpec(memory_space=pltpu.VMEM)
    hbm = pl.BlockSpec(memory_space=pl.ANY)
    dma = pltpu.SemaphoreType.DMA
    result = jax.ShapeDtypeStruct((TOK, D), BF16)
    first_out, input_grads = pl.pallas_call(
        kernel,
        out_shape=(result, result),
        in_specs=[vmem] * 4 + [hbm] * 6,
        out_specs=(hbm, hbm),
        scratch_shapes=[
            pltpu.VMEM((3, TOK, D), BF16),
            pltpu.VMEM((3, HID, D), BF16),
            pltpu.VMEM((2, 8, TOK), F32),
            pltpu.VMEM((2, 8, TOK), F32),
            pltpu.VMEM((3, EXPERTS * BLK, W), BF16),
            pltpu.VMEM((3, 2, ROWS, W), BF16),
            pltpu.VMEM((2, 2, ROWS, W), BF16),
            pltpu.VMEM((2, 4, 4 * BLK, W), BF16),
            pltpu.VMEM((2, 8, BLK, W), BF16),
            pltpu.VMEM((2, EXPERTS * BLK, W), BF16),
            pltpu.VMEM((2, 3, ROWS, HID), F32),
            pltpu.VMEM((2, ROWS, HID), BF16),
            pltpu.VMEM((PIECES, PIECE, D), BF16),
            dma((3,)),
            dma((2,)),
            dma((2,)),
            dma((3, EXPERTS)),
            dma((3, 8)),
            dma((3, 16)),
            dma((3, SRC)),
            dma((2, 4)),
            dma((2, 4)),
            dma((2, 8)),
            dma((2, 8)),
            dma((2, 8)),
            dma((2, EXPERTS)),
            dma((PIECES,)),
            dma((PIECES,)),
            dma((PIECES,)),
            dma((2, 2)),
        ],
        compiler_params=pltpu.CompilerParams(
            collective_id=0, has_side_effects=True, vmem_limit_bytes=63 * 1024 * 1024
        ),
    )(
        first_routes.reshape(1, TOK),
        first_probs.reshape(1, TOK),
        second_routes.reshape(1, TOK),
        second_probs.reshape(1, TOK),
        first_acts[0],
        second_acts[0],
        second_grads[0],
        gate_weight[0].T,
        up_weight[0].T,
        down_weight[0],
    )
    return (first_out[None], input_grads[None])


def solution(mesh):
    in_specs = (
        P("pipe", "ep", None),
        P("pipe", "ep", None),
        P("pipe", "ep", None),
        P("pipe", "ep", None),
        P("pipe", "ep", None),
        P("pipe", "ep", None),
        P("pipe", "ep", None),
        P("pipe", None, "ep"),
        P("pipe", None, "ep"),
        P("pipe", "ep", None),
    )
    out_specs = (P("pipe", "ep", None), P("pipe", "ep", None))
    return jax.shard_map(body, mesh=mesh, in_specs=in_specs, out_specs=out_specs, check_vma=False)
```

time: 244 us -> 233 us (0.955)
  the two profiles are of different devices: /device:TPU:200 before, /device:TPU:7 now
where the time goes in v3:
time: 233 us; the launch traced here: 231 us
  Pallas kernels  227 us (97%)
  local copies, waits for them, and re-layouts  3.35 us (1%)
    pallas_call x1, Pallas kernels, body(): pl.pallas_call(kernel, out_shape=(result, result), in_specs=[vmem] * 4 +...  227 us

profile of v3, /device:TPU:7, one launch (start us, length us, event | category | flops | bytes accessed | tf_op | source)
XLA Modules:
  0.0 231.0 jit_solution(4475574278909738879)
XLA Ops:
  0.6 227.0 %shard_map.113 = (bf16[128,4096]{1,0:T(8,128)(2,1)}, bf16[128,4096]{1,0:T(8,128)(2,1)}) custom-call(s32[1,128]{1,0:T(1,128)} %bitcast.24, f32[1,128]{1,0:T(1,128)} %bitcast.25, s32[1,128]{1,0:T(1,128)} %bitcast.26, f32[1,128]{1,0:T(1,128)} %bitcast.27, bf16[128,4096]{1,0:T(8,128)(2,1)} %bitcast.19, bf16[128,4096]{1,0:T(8,128)(2,1)} %bitcast.20, ...), custom_call_target="tpu_custom_call" | custom-call | tf_op jit(solution)/shard_map/pallas_call | solution.py:577
  227.7 0.0 copy-start
  227.7 2.4 %copy.14 = bf16[1,128,4096]{2,1,0:T(8,128)(2,1)} copy(bf16[1,128,4096]{2,1,0:T(8,128)(2,1)} %bitcast.23) | data formatting | bytes 2097152
  230.0 0.0 copy-done
  230.0 1.0 copy.15
Async XLA Ops:
  227.7 2.4 %copy-start = (bf16[128,4096]{1,0:T(8,128)(2,1)S(1)}, bf16[128,4096]{1,0:T(8,128)(2,1)}, u32[]{:S(2)}) copy-start(bf16[128,4096]{1,0:T(8,128)(2,1)} %get-tuple-element.5) | copy-start | bytes 3145732

commit v4 on v3

--- a/solution.py
+++ b/solution.py
@@ -16,6 +16,7 @@
 EXPERTS = 8
 KB = 512
 NK = D // KB
+WIDE = 1024
 W = D + KB
 BLK = 16
 SRC = 32
@@ -37,6 +38,10 @@
 
 def cols(index):
     return pl.ds(pl.multiple_of(index * KB, KB), KB)
+
+
+def wide(index):
+    return pl.ds(pl.multiple_of(index * WIDE, WIDE), WIDE)
 
 
 def iota(shape, dim):
@@ -325,12 +330,12 @@
         acc[h, 0:2] = jnp.zeros((2, ROWS, HID), F32)
 
         def step(k, carry):
-            values = recv[d, h, :, cols(k)]
-            acc[h, 0] += lax.dot_general(values, held_w[0, :, cols(k)], NT, preferred_element_type=F32)
-            acc[h, 1] += lax.dot_general(values, held_w[1, :, cols(k)], NT, preferred_element_type=F32)
-            return carry
-
-        lax.fori_loop(0, NK, step, 0)
+            values = recv[d, h, :, wide(k)]
+            acc[h, 0] += lax.dot_general(values, held_w[0, :, wide(k)], NT, preferred_element_type=F32)
+            acc[h, 1] += lax.dot_general(values, held_w[1, :, wide(k)], NT, preferred_element_type=F32)
+            return carry
+
+        lax.fori_loop(0, D // WIDE, step, 0)
 
     def forward_compute(h):
         gate_up(ONE, h)
@@ -338,10 +343,10 @@
         hid[0] = (gate * jax.nn.sigmoid(gate) * acc[h, 1]).astype(BF16)
 
         def step(k, carry):
-            part[0, h, :, cols(k)] = jnp.dot(hid[0], held_w[2, :, cols(k)], preferred_element_type=F32).astype(BF16)
-            return carry
-
-        lax.fori_loop(0, NK, step, 0)
+            part[0, h, :, wide(k)] = jnp.dot(hid[0], held_w[2, :, wide(k)], preferred_element_type=F32).astype(BF16)
+            return carry
+
+        lax.fori_loop(0, D // WIDE, step, 0)
         fold(0, h)
 
     def backward_hidden(h):
@@ -349,10 +354,10 @@
         acc[h, 2] = jnp.zeros((ROWS, HID), F32)
 
         def down(k, carry):
-            acc[h, 2] += lax.dot_general(recv[GRADS, h, :, cols(k)], held_w[2, :, cols(k)], NT, preferred_element_type=F32)
-            return carry
-
-        lax.fori_loop(0, NK, down, 0)
+            acc[h, 2] += lax.dot_general(recv[GRADS, h, :, wide(k)], held_w[2, :, wide(k)], NT, preferred_element_type=F32)
+            return carry
+
+        lax.fori_loop(0, D // WIDE, down, 0)
         gate = acc[h, 0]
         sig = jax.nn.sigmoid(gate)
         slope = acc[h, 2] * sig
@@ -361,12 +366,12 @@
 
     def backward_rows(h):
         def step(k, carry):
-            total = jnp.dot(hid[0], held_w[0, :, cols(k)], preferred_element_type=F32)
-            total = total + jnp.dot(hid[1], held_w[1, :, cols(k)], preferred_element_type=F32)
-            part[1, h, :, cols(k)] = total.astype(BF16)
-            return carry
-
-        lax.fori_loop(0, NK, step, 0)
+            total = jnp.dot(hid[0], held_w[0, :, wide(k)], preferred_element_type=F32)
+            total = total + jnp.dot(hid[1], held_w[1, :, wide(k)], preferred_element_type=F32)
+            part[1, h, :, wide(k)] = total.astype(BF16)
+            return carry
+
+        lax.fori_loop(0, D // WIDE, step, 0)
         fold(1, h)
 
     def to_core(m, half, parity):

time: 233 us -> 227 us (0.974)
  Pallas kernels: 227 us -> 223 us
    pallas_call x1, Pallas kernels: 227 us -> 223 us  [body(): pl.pallas_call(kernel, out_shape=(result, result), in_specs=[vmem] * 4 +...]
where the time goes in v4:
time: 227 us
  Pallas kernels  223 us (98%)
  local copies, waits for them, and re-layouts  3.35 us (1%)
    pallas_call x1, Pallas kernels, body(): pl.pallas_call(kernel, out_shape=(result, result), in_specs=[vmem] * 4 +...  223 us

profile of v4, /device:TPU:7, one launch (start us, length us, event | category | flops | bytes accessed | tf_op | source)
XLA Modules:
  0.0 226.6 jit_solution(17311792217470309308)
XLA Ops:
  0.6 222.6 %shard_map.113 = (bf16[128,4096]{1,0:T(8,128)(2,1)}, bf16[128,4096]{1,0:T(8,128)(2,1)}) custom-call(s32[1,128]{1,0:T(1,128)} %bitcast.24, f32[1,128]{1,0:T(1,128)} %bitcast.25, s32[1,128]{1,0:T(1,128)} %bitcast.26, f32[1,128]{1,0:T(1,128)} %bitcast.27, bf16[128,4096]{1,0:T(8,128)(2,1)} %bitcast.19, bf16[128,4096]{1,0:T(8,128)(2,1)} %bitcast.20, ...), custom_call_target="tpu_custom_call" | custom-call | tf_op jit(solution)/shard_map/pallas_call | solution.py:582
  223.2 0.0 copy-start
  223.2 2.4 %copy.14 = bf16[1,128,4096]{2,1,0:T(8,128)(2,1)} copy(bf16[1,128,4096]{2,1,0:T(8,128)(2,1)} %bitcast.23) | data formatting | bytes 2097152
  225.6 0.0 copy-done
  225.6 1.0 copy.15
Async XLA Ops:
  223.2 2.4 %copy-start = (bf16[128,4096]{1,0:T(8,128)(2,1)S(1)}, bf16[128,4096]{1,0:T(8,128)(2,1)}, u32[]{:S(2)}) copy-start(bf16[128,4096]{1,0:T(8,128)(2,1)} %get-tuple-element.5) | copy-start | bytes 3145732

commit v5 on v4

--- a/solution.py
+++ b/solution.py
@@ -79,7 +79,7 @@
 
 def kernel(
     routes_one, probs_one, routes_two, probs_two, one_hbm, acts_hbm, grads_hbm, gate_hbm, up_hbm, down_hbm,
-    out_one, out_two,
+    out,
     held, held_w, meta_out, meta_in, stage, recv, part, cx, px, home, acc, hid, relay,
     load_sem, msend, mrecv, dsend, fsend, csend, rsem, xsend, xrecv, psend, precv, hsend, hrecv,
     wsend, wrecv, relay_recv, out_sem,
@@ -124,14 +124,14 @@
         @pl.when(c == 0)
         def _():
             pltpu.make_async_remote_copy(
-                src, held_w.at[i, part_of], wsend.at[t], wrecv.at[t],
+                src, held_w.at[i, part_of], wsend.at[0], wrecv.at[t],
                 device_id=(p, round_x * 8 + round_z * 2), device_id_type=MESH,
             ).start()
 
         @pl.when(jnp.logical_and(c == 1, jnp.logical_not(even)))
         def _():
             pltpu.make_async_remote_copy(
-                src, relay.at[t], wsend.at[t], relay_recv.at[t], device_id=(p, beside), device_id_type=MESH
+                src, relay.at[t], wsend.at[0], relay_recv.at[t], device_id=(p, beside), device_id_type=MESH
             ).start()
 
     def give_all(i):
@@ -148,7 +148,7 @@
             pltpu.make_async_remote_copy(
                 relay.at[t],
                 held_w.at[t // SPLIT, pl.ds(pl.multiple_of((t % SPLIT) * PIECE, BLK), PIECE)],
-                wsend.at[t],
+                wsend.at[0],
                 wrecv.at[t],
                 device_id=(p, beyond),
                 device_id_type=MESH,
@@ -238,17 +238,6 @@
         def _():
             pltpu.make_async_copy(src, dst, sem).start()
 
-    def sent(move, may_stay):
-        target, src, dst, send_sem, sem, device = move
-
-        def wait():
-            pltpu.make_async_remote_copy(src, dst, send_sem, sem, device_id=device, device_id_type=MESH).wait_send()
-
-        if may_stay:
-            pl.when(target != j)(wait)
-        else:
-            wait()
-
     def dispatch(d, i):
         half = i // 4
         to_z = flip(z, i % 4 if d == ACTS else 3 - i % 4)
@@ -258,7 +247,7 @@
         b = place(x % 2, c, z)
         sem = rsem.at[d, half * HALF + b]
         src, dst = stage.at[d, rows16(e)], recv.at[d, half, rows16(b)]
-        return target, src, dst, dsend.at[d, i], sem, (section[d], target)
+        return target, src, dst, dsend.at[d], sem, (section[d], target)
 
     def send(d, low, high):
         def step(i, carry):
@@ -278,10 +267,10 @@
         )
 
     def to_pair_sem(d, half, source_z):
-        return fsend.at[d, half * 4 + source_z]
+        return fsend.at[d]
 
     def to_core_sem(d, half, parity, source_z):
-        return csend.at[d, half * 8 + parity * 4 + source_z]
+        return csend.at[d]
 
     def forward(d, half, direct, give=None, relay_of=None):
         parity = enters(half) if direct else 1 - enters(half)
@@ -398,7 +387,7 @@
         return pltpu.make_async_remote_copy(
             part.at[m, half, rows16(place(1 - enters(half), c, source_z))],
             px.at[m, n],
-            psend.at[m, n],
+            psend.at[m],
             precv.at[m, n],
             device_id=(p, pair),
             device_id_type=MESH,
@@ -408,7 +397,7 @@
         b = place(enters(half), c, source_z)
         target = (x if half == 0 else 3 - x) * 8 + source_z * 2 + c
         src, dst, sem = part.at[m, half, rows16(b)], home.at[m, rows16(expert)], hrecv.at[m, expert]
-        return target, src, dst, hsend.at[m, half * 4 + source_z], sem, (p, target)
+        return target, src, dst, hsend.at[m], sem, (p, target)
 
     def return_first(m, half):
         for parity, leaves in ((1 - enters(half), False), (enters(half), True)):
@@ -435,48 +424,29 @@
 
         lax.fori_loop(0, 4, step, 0)
 
+    def all_sent(ref, sem):
+        pltpu.make_async_remote_copy(ref, ref, sem, sem, device_id=(p, other), device_id_type=MESH).wait_send()
+
     def drain_dispatch(d):
-        def injected(i, carry):
-            sent(dispatch(d, i), d == ACTS)
-            return carry
-
-        lax.fori_loop(0, EXPERTS, injected, 0)
-        for half in range(2):
-
-            def passed(k, carry):
-                onward(d, half, place(enters(half), c, k), pair, to_pair_sem(d, half, k)).wait_send()
-                for parity in range(2):
-                    onward(d, half, place(parity, c, k), other, to_core_sem(d, half, parity, k)).wait_send()
-                return carry
-
-            lax.fori_loop(0, 4, passed, 0)
+        all_sent(stage.at[d, pl.ds(0, (7 if d == ACTS else 8) * BLK)], dsend.at[d])
+        all_sent(recv.at[d, 0, pl.ds(0, 8 * BLK)], fsend.at[d])
+        all_sent(recv.at[d, 0, pl.ds(0, 16 * BLK)], csend.at[d])
 
     def drain_return(m):
         for half in range(2):
             to_core(m, half, 0).wait_send()
             to_core(m, half, 1).wait_send()
-
-            def returned(k, carry):
-                to_pair(m, half, k).wait_send()
-                sent(to_home(m, half, k), half == 0)
-                return carry
-
-            lax.fori_loop(0, 4, returned, 0)
+        all_sent(part.at[m, 0, pl.ds(0, 8 * BLK)], psend.at[m])
+        all_sent(part.at[m, 0, pl.ds(0, 7 * BLK)], hsend.at[m])
 
     def drain_weights():
-        def gone(t, carry):
-            pltpu.make_async_remote_copy(
-                relay.at[t], relay.at[t], wsend.at[t], wrecv.at[t], device_id=(p, beside), device_id_type=MESH
-            ).wait_send()
-            return carry
-
-        lax.fori_loop(0, PIECES, gone, 0)
-
-    def result(m, n, out):
+        all_sent(relay, wsend.at[0])
+
+    def result(m, n):
         part_of = pl.ds(n * (D // 2), D // 2)
-        return pltpu.make_async_copy(held.at[m, :, part_of], out.at[:, part_of], out_sem.at[m, n])
-
-    def collect(m, main_col, tail_col, prob_col, out):
+        return pltpu.make_async_copy(held.at[m, :, part_of], out.at[m, :, part_of], out_sem.at[m, n])
+
+    def collect(m, main_col, tail_col, prob_col):
         def step(e, carry):
             pltpu.make_async_copy(home.at[m, rows16(e)], home.at[m, rows16(e)], hrecv.at[m, e]).wait()
             return carry
@@ -492,7 +462,7 @@
                 got = prob_col * got
             held[m, :, k * KB : (k + 1) * KB] = got.astype(BF16)
             if k % 4 == 3:
-                result(m, k // 4, out).start()
+                result(m, k // 4).start()
 
     loads[0].wait()
     fill(ACTS, main_row_two, tail_row_two, None)
@@ -555,12 +525,12 @@
         copy.wait_send()
     return_second(1, 1)
     drain_return(0)
-    collect(0, main_col_one, tail_col_one, column(probs_one[...]), out_one)
-    collect(1, main_col_two, tail_col_two, None, out_two)
+    collect(0, main_col_one, tail_col_one, column(probs_one[...]))
+    collect(1, main_col_two, tail_col_two, None)
     drain_return(1)
     for n in range(2):
-        result(0, n, out_one).wait()
-        result(1, n, out_two).wait()
+        result(0, n).wait()
+        result(1, n).wait()
 
 
 def body(
@@ -578,12 +548,11 @@
     vmem = pl.BlockSpec(memory_space=pltpu.VMEM)
     hbm = pl.BlockSpec(memory_space=pl.ANY)
     dma = pltpu.SemaphoreType.DMA
-    result = jax.ShapeDtypeStruct((TOK, D), BF16)
-    first_out, input_grads = pl.pallas_call(
+    both = pl.pallas_call(
         kernel,
-        out_shape=(result, result),
+        out_shape=jax.ShapeDtypeStruct((2, TOK, D), BF16),
         in_specs=[vmem] * 4 + [hbm] * 6,
-        out_specs=(hbm, hbm),
+        out_specs=hbm,
         scratch_shapes=[
             pltpu.VMEM((3, TOK, D), BF16),
             pltpu.VMEM((3, HID, D), BF16),
@@ -601,17 +570,17 @@
             dma((3,)),
             dma((2,)),
             dma((2,)),
-            dma((3, EXPERTS)),
-            dma((3, 8)),
-            dma((3, 16)),
+            dma((3,)),
+            dma((3,)),
+            dma((3,)),
             dma((3, SRC)),
             dma((2, 4)),
             dma((2, 4)),
+            dma((2,)),
             dma((2, 8)),
-            dma((2, 8)),
-            dma((2, 8)),
+            dma((2,)),
             dma((2, EXPERTS)),
-            dma((PIECES,)),
+            dma((1,)),
             dma((PIECES,)),
             dma((PIECES,)),
             dma((2, 2)),
@@ -631,7 +600,7 @@
         up_weight[0].T,
         down_weight[0],
     )
-    return (first_out[None], input_grads[None])
+    return (both[0:1], both[1:2])
 
 
 def solution(mesh):

time: 227 us -> 225 us (level)
    unnamed x4 -> x0, local copies, waits for them, and re-layouts: 3.35 us -> none
    slice x0 -> x1, local copies, waits for them, and re-layouts: none -> 3.08 us  [body(): return (both[0:1], both[1:2])]
where the time goes in v5:
time: 225 us
  Pallas kernels  221 us (98%)
  local copies, waits for them, and re-layouts  3.08 us (1%)
    pallas_call x1, Pallas kernels, body(): pl.pallas_call(kernel, out_shape=jax.ShapeDtypeStruct((2, TOK, D), BF16),...  221 us

profile of v5, /device:TPU:7, one launch (start us, length us, event | category | flops | bytes accessed | tf_op | source)
XLA Modules:
  0.0 225.2 jit_solution(8166466205369255679)
XLA Ops:
  0.6 221.5 %shard_map.113 = bf16[2,128,4096]{2,1,0:T(8,128)(2,1)} custom-call(s32[1,128]{1,0:T(1,128)} %bitcast.20, f32[1,128]{1,0:T(1,128)} %bitcast.21, s32[1,128]{1,0:T(1,128)} %bitcast.22, f32[1,128]{1,0:T(1,128)} %bitcast.23, bf16[128,4096]{1,0:T(8,128)(2,1)} %bitcast.17, bf16[128,4096]{1,0:T(8,128)(2,1)} %bitcast.18, bf16[128,4096]{1,0:T(8,128)(2,1)} %bitcast.19, ...), custom_call_target="tpu_custom_call" | custom-call | tf_op jit(solution)/shard_map/pallas_call | solution.py:551
  222.1 3.1 %fusion = (bf16[1,128,4096]{2,1,0:T(8,128)(2,1)}, bf16[1,128,4096]{2,1,0:T(8,128)(2,1)}) fusion(bf16[2,128,4096]{2,1,0:T(8,128)(2,1)} %shard_map.113), kind=kLoop, calls=%fused_computation | loop fusion | bytes 4194304 | tf_op jit(solution)/shard_map/slice | solution.py:603
